TPU v7x, 256 devices: a whole 4x4x8 slice. The times are simulated.
256 devices in a mesh: comp: 4 (over z_hi), lat: 4 (over x), lon: 16 (over z_lo, y, core).
Axes of the slice: x: 4, y: 4, z: 8 (z_hi: 4, z_lo: 2; z = z_hi * 2 + z_lo), core: 2. Of those that a mesh axis runs over, the one named last changes fastest.
Arguments:
- checkpoint: float32 [4, 6, 2, 256, 4096], P('comp', None, None, 'lat', 'lon'), may hold values from -6 to 6
- adjoint_in: float32 [4, 6, 2, 256, 4096], P('comp', None, None, 'lat', 'lon'), may hold values from -6 to 6
- land_mask: int32 [256, 4096], P('lat', 'lon'), may hold values 0 or 1
- diffusivity: float32 [6], replicated, may hold values from 0.02 to 0.2
- penetration: float32 [6], replicated, may hold values from 0.2 to 1
- column_weight: float32 [4, 192], replicated, may hold values from -0.4375 to 0.4375
- routes: int32 [16384, 1], P(('lat', 'lon')), may hold values from 0 to 63; in each aligned block of 256 rows (0 to 255, 256 to 511, ...) at most 8 rows name the same one
- dest_row: int32 [16384], P(('lat', 'lon')), may hold values from 0 to 63
- weight_id: int32 [16384], P(('lat', 'lon')), may hold values from 0 to 7
- regrid_table: float32 [8, 4], replicated, may hold values from 0.25 to 1
Outputs:
- adjoint_out: float32 [4, 6, 2, 256, 4096], P('comp', None, None, 'lat', 'lon')
Inputs may be any that keep to these rules, and one draw needn't show every extreme that they name: `routes`: among the rows of one atmosphere tile no ocean tile is named more than 8 times, a bound that some block reaches.
All inputs are finite; a program needn't handle non-finite values. No bound on the sum of `land_mask` on one device may be relied on, other than what follows from the above.
Results may differ from a plain program's by a relative error of at most 0.00011.
Values sent between devices are 32-bit elements; how exact they have to be, the bound alone decides.
No kernel may reach another device: no remote copies, remote signals or barrier semaphores. Data moves between devices by JAX's collectives and lax.ppermute only.
A program may use at most 64 MiB of HBM per device.

v0:
```python
import jax
import jax.numpy as jnp
from jax import lax
from jax.experimental import pallas as pl
from jax.experimental.pallas import tpu as pltpu
from jax.sharding import PartitionSpec as P

NSTEP = 4
STEP_COEF = 0.2
SPEED_BASE = 0.5
SPEED_GAIN = 0.5

FLD = 6
NFLUX = 4
LEVB = 2
ROWS = 64
COLS = 256
PLANES = FLD * LEVB
HALO_ROWS = 80
ADJ_ROWS = 72
WIDE = 384
LANES = 128
TILES = 64
SEGS = 16
FAR = -1.0

f32 = jnp.float32
bf16 = jnp.bfloat16
VM = pltpu.VMEM
SM = pltpu.SMEM


def vmem():
    return pl.BlockSpec(memory_space=VM)


def smem():
    return pl.BlockSpec(memory_space=SM)


def in_vmem(shape, dtype=f32):
    return VM(shape, dtype)


def east(x):
    return pltpu.roll(x, WIDE - 1, 1)


def west(x):
    return pltpu.roll(x, 1, 1)


def north(x):
    return pltpu.roll(x, x.shape[0] - 1, 0)


def south(x):
    return pltpu.roll(x, 1, 0)


def iota(shape, dim):
    return lax.broadcasted_iota(jnp.int32, shape, dim)


def split(x):
    high = x.astype(bf16)
    return high, (x - high.astype(f32)).astype(bf16)


def dot(x, y):
    return jnp.dot(x, y, preferred_element_type=f32)


def flux_kernel(place, checkpoint, adjoint_in, mask, weight, flux, to_north, to_south):
    for plane in range(PLANES):
        f, l = plane // LEVB, plane % LEVB
        to_north[plane] = checkpoint[f, l, ROWS - 8 : ROWS, :]
        to_south[plane] = checkpoint[f, l, 0:8, :]
        to_north[PLANES + plane] = adjoint_in[f, l, ROWS - 8 : ROWS, :]
        to_south[PLANES + plane] = adjoint_in[f, l, 0:8, :]
    to_north[2 * PLANES] = mask[ROWS - 8 : ROWS, :].astype(f32)
    to_south[2 * PLANES] = mask[0:8, :].astype(f32)

    @pl.when(place[0] == 3)
    def _():
        t = jnp.tanh(checkpoint[...])
        sens = (adjoint_in[...] * (1.0 - t * t)).reshape(PLANES * ROWS, COLS)
        by_kind = jnp.dot(weight[...], sens, precision=lax.Precision.HIGHEST, preferred_element_type=f32)
        rows = []
        for q in range(4):
            rows.append(
                jnp.concatenate(
                    [by_kind[k * 4 : k * 4 + 4, q * 64 : q * 64 + 64] for k in range(NFLUX)], axis=1
                )
            )
        by_seg = jnp.concatenate(rows, axis=0)
        flux[0:16, :] = by_seg[:, 0:LANES]
        flux[16:32, :] = by_seg[:, LANES:]

    @pl.when(place[0] != 3)
    def _():
        flux[...] = jnp.zeros((32, LANES), f32)


def strip_kernel(checkpoint, adjoint_in, mask, from_south, from_north, to_east, to_west):
    lane_group = iota((HALO_ROWS, LANES), 1) // 8
    for kind, source in enumerate((checkpoint, adjoint_in)):
        east_strip = jnp.zeros((HALO_ROWS, LANES), f32)
        west_strip = jnp.zeros((HALO_ROWS, LANES), f32)
        for plane in range(PLANES + 1 - kind):
            if plane < PLANES:
                f, l = plane // LEVB, plane % LEVB
                at = kind * PLANES + plane
                own_w, own_e = source[f, l, :, 0:LANES], source[f, l, :, LANES:]
            else:
                at = 2 * PLANES
                own_w, own_e = mask[:, 0:LANES].astype(f32), mask[:, LANES:].astype(f32)
            edge_w = jnp.concatenate([own_w, from_north[at, :, 0:LANES], from_south[at, :, 0:LANES]], axis=0)
            edge_e = jnp.concatenate([own_e, from_north[at, :, LANES:], from_south[at, :, LANES:]], axis=0)
            east_strip = jnp.where(lane_group == plane, pltpu.roll(edge_e, 8 * plane + 8, 1), east_strip)
            moved = edge_w if plane == 0 else pltpu.roll(edge_w, 8 * plane, 1)
            west_strip = jnp.where(lane_group == plane, moved, west_strip)
        to_east[kind] = east_strip
        to_west[kind] = west_strip


def to_adjoint_rows(x):
    row = iota((8, WIDE), 0)
    return jnp.concatenate([x[0:ROWS], jnp.where(row < 4, x[ROWS : ROWS + 8], x[ROWS + 8 :])], axis=0)


def forward_kernel(
    place,
    diffusivity,
    checkpoint,
    adjoint_in,
    mask,
    from_south,
    from_north,
    from_west,
    from_east,
    wet_out,
    start,
    speed_e,
    speed_n,
    grad_e,
    grad_n,
    early_e,
    early_n,
    base,
    state,
    wet_all,
    spare,
    spare_e,
    spare_n,
):
    @pl.when(place[0] == 3)
    def _():
        t = jnp.tanh(checkpoint[...])
        base[...] = adjoint_in[...] * (1.0 - t * t)

    @pl.when(place[0] != 3)
    def _():
        lane = iota((HALO_ROWS, LANES), 1)

        def widened(own, at, kind, plane):
            full = jnp.concatenate([own, from_north[at], from_south[at]], axis=0)
            low, high = from_east[kind], from_west[kind]
            if plane:
                low = pltpu.roll(low, LANES - 8 * plane, 1)
            high = pltpu.roll(high, (120 - 8 * plane) % LANES, 1)
            edge = jnp.where(lane < 8, low, jnp.where(lane >= 120, high, 0.0))
            return jnp.concatenate([full, edge], axis=1)

        wet = widened(mask[...].astype(f32), 2 * PLANES, 0, PLANES)
        wet_all[...] = wet
        wet_out[...] = to_adjoint_rows(wet)
        for f in range(FLD):
            for l in range(LEVB):
                plane = f * LEVB + l
                state[0, plane] = widened(checkpoint[f, l], plane, 0, plane)
                adj = to_adjoint_rows(widened(adjoint_in[f, l], PLANES + plane, 1, plane))
                if f < NFLUX:
                    start[f, l] = adj
                else:
                    spare[f - NFLUX, l] = adj

        def sweep(step, last):
            now, later = step % 2, (step + 1) % 2
            for l in range(LEVB):
                a = 0.5 * STEP_COEF * (SPEED_BASE + SPEED_GAIN * state[now, l])
                b = (0.5 * STEP_COEF * SPEED_GAIN) * state[now, LEVB + l]
                speed_e[step, l] = to_adjoint_rows(a)
                speed_n[step, l] = to_adjoint_rows(b)
                for f in range(FLD):
                    d = diffusivity[f]
                    q = state[now, f * LEVB + l]
                    q_e, q_w, q_n, q_s = east(q), west(q), north(q), south(q)
                    across, along = q_e - q_w, q_n - q_s
                    half = -0.5 * STEP_COEF * SPEED_GAIN
                    if f < NFLUX:
                        grad_e[step, f, l] = to_adjoint_rows(half * across)
                        grad_n[step, f, l] = to_adjoint_rows(half * along)
                    else:
                        spare_e[step, f - NFLUX, l] = to_adjoint_rows(half * across)
                        spare_n[step, f - NFLUX, l] = to_adjoint_rows(half * along)
                    if not last:
                        moved = (1.0 - 4.0 * d) * q + d * ((q_e + q_w) + (q_n + q_s)) - a * across - b * along
                        state[later, f * LEVB + l] = wet_all[...] * moved

        for step in range(NSTEP):
            sweep(step, step + 1 == NSTEP)

        for step in reversed(range(NSTEP)):
            for l in range(LEVB):
                a, b, w = speed_e[step, l], speed_n[step, l], wet_out[...]
                sum_e, sum_n = 0.0, 0.0
                for f in range(FLD - NFLUX):
                    d = diffusivity[NFLUX + f]
                    mu = w * spare[f, l]
                    sum_e = sum_e + mu * spare_e[step, f, l]
                    sum_n = sum_n + mu * spare_n[step, f, l]
                    spare[f, l] = pulled(mu, a, b, d)
                early_e[step, l] = sum_e
                early_n[step, l] = sum_n
        for f in range(FLD - NFLUX):
            for l in range(LEVB):
                base[NFLUX + f, l] = spare[f, l, 0:ROWS, 0:COLS]


def pulled(mu, a, b, d):
    mixed, carried_e, carried_n = d * mu, a * mu, b * mu
    return (
        (1.0 - 4.0 * d) * mu
        + (east(mixed + carried_e) + west(mixed - carried_e))
        + (north(mixed + carried_n) + south(mixed - carried_n))
    )


def route_kernel(place, table, routing, high, low, spread_own, spread_side, code_t, prof_t, total):
    lat_me, lon_me = place[1], place[2]

    def listed(at):
        return jnp.concatenate(
            [routing[pl.ds(2 * at, TILES, stride=8), :], routing[pl.ds(2 * at + 1, TILES, stride=8), :]], axis=0
        )

    dest, row, profile = listed(0), listed(1), listed(2)
    dest_lat, dest_lon = dest // 16, dest % 16
    row = row + ROWS * (dest_lat - lat_me)
    valid = jnp.logical_and(row >= -4, row < ROWS + 4)
    code = jnp.where(row < 0, row + ADJ_ROWS, row).astype(f32)
    for way in range(3):
        lon_of = (lon_me + (0, 1, 15)[way]) % 16
        here = jnp.logical_and(valid, dest_lon == lon_of)
        code_t[way] = jnp.where(here, code, FAR).T
    for c in range(4):
        weights = jnp.zeros((LANES, LANES), f32)
        for w in range(8):
            weights = jnp.where(profile == w, table[w, c], weights)
        prof_t[c] = weights.T
    rows = iota((ADJ_ROWS, LANES), 0).astype(f32)

    def build(step, carry):
        way, seg = step // 8, step % 8
        sums = [jnp.zeros((ADJ_ROWS, LANES), f32) for _ in range(4)]
        for r in range(16):
            at = seg * 16 + r
            hit = code_t[way, pl.ds(at, 1), :] == rows
            for c in range(4):
                sums[c] = sums[c] + jnp.where(hit, prof_t[c, pl.ds(at, 1), :], 0.0)
        for c in range(4):
            total[seg, way * 4 + c] = sums[c]
        return carry

    lax.fori_loop(0, 24, build, 0)
    for seg in range(8):
        whole = total[seg].reshape(12 * ADJ_ROWS, LANES)
        head, tail = split(whole)
        high[:, seg * LANES : (seg + 1) * LANES] = head
        low[:, seg * LANES : (seg + 1) * LANES] = tail

    src, out = iota((512, 512), 0), iota((512, 512), 1)
    same = (src // 64) % 2 == out // COLS
    spread_own[...] = jnp.where(jnp.logical_and(same, out % COLS == 4 * (src % 64) + src // 128), 1.0, 0.0).astype(bf16)
    src, out = iota((512, 256), 0), iota((512, 256), 1)
    same = (src // 64) % 2 == out // LANES
    first = jnp.logical_and(src % 64 == 0, out % LANES == src // 128)
    final = jnp.logical_and(src % 64 == 63, out % LANES == 124 + src // 128)
    spread_side[...] = jnp.where(jnp.logical_and(same, jnp.logical_or(first, final)), 1.0, 0.0).astype(bf16)


def adjoint_kernel(
    place,
    diffusivity,
    penetration,
    gathered,
    high,
    low,
    spread_own,
    spread_side,
    wet,
    start,
    speed_e,
    speed_n,
    grad_e,
    grad_n,
    early_e,
    early_n,
    base,
    out,
    g_high,
    g_low,
    lam,
    done,
    sem,
):
    del base

    @pl.when(place[0] != 3)
    def _():
        for seg in range(8):
            for h in range(2):
                s = h * 8 + seg
                at = (s % 4) * 4 + s // 4
                for half in range(2):
                    part = gathered[pl.ds(half * 16 + at, TILES, stride=32), :]
                    head, tail = split(part)
                    rows = slice(seg * LANES + h * 64, seg * LANES + h * 64 + 64)
                    g_high[rows, half * LANES : (half + 1) * LANES] = head
                    g_low[rows, half * LANES : (half + 1) * LANES] = tail
        coarse = dot(high[...], g_high[...]) + dot(high[...], g_low[...]) + dot(low[...], g_high[...])
        own_parts, side_parts = [], []
        lane = iota((ADJ_ROWS, LANES), 1) % 64
        for half in range(2):
            cols = slice(half * LANES, (half + 1) * LANES)

            def piece(way, c):
                at = (way * 4 + c) * ADJ_ROWS
                return coarse[at : at + ADJ_ROWS, cols]

            own = jnp.concatenate([piece(0, c) for c in range(4)], axis=1)
            side = jnp.concatenate(
                [jnp.where(lane == 0, piece(1, c), jnp.where(lane == 63, piece(2, c), 0.0)) for c in range(4)], axis=1
            )
            for parts, value in ((own_parts, own), (side_parts, side)):
                head = value.astype(bf16).astype(f32)
                parts += [head, value - head]
        own = dot(jnp.concatenate(own_parts, axis=0).astype(bf16), spread_own[...])
        side = dot(jnp.concatenate(side_parts, axis=0).astype(bf16), spread_side[...])
        w = wet[...]
        band = jnp.minimum(place[0], 2)
        for k in range(NFLUX):
            at, sub = (k // 2) * 2 * ADJ_ROWS, k % 2
            own_k = own[:, sub * COLS : (sub + 1) * COLS]
            side_k = side[:, sub * LANES : (sub + 1) * LANES]
            whole = jnp.concatenate(
                [x[at : at + ADJ_ROWS] + x[at + ADJ_ROWS : at + 2 * ADJ_ROWS] for x in (own_k, side_k)], axis=1
            )
            forcing = w * whole
            for l in range(LEVB):
                lam[k, l] = start[k, l] + penetration[band * LEVB + l] * forcing

        def back(i, carry):
            step = NSTEP - 1 - i
            for l in range(LEVB):
                a, b, w = speed_e[step, l], speed_n[step, l], wet[...]
                sum_e, sum_n = early_e[step, l], early_n[step, l]
                for f in (2, 3, 1, 0):
                    mu = w * lam[f, l]
                    sum_e = sum_e + mu * grad_e[step, f, l]
                    sum_n = sum_n + mu * grad_n[step, f, l]
                    lam[f, l] = pulled(mu, a, b, diffusivity[f])
                lam[0, l] = lam[0, l] + sum_e
                lam[1, l] = lam[1, l] + sum_n
            return carry

        lax.fori_loop(0, NSTEP, back, 0)
        for k in range(NFLUX):
            for l in range(LEVB):
                done[k, l] = lam[k, l, 0:ROWS, 0:COLS]
        copy = pltpu.make_async_copy(done, out.at[0:NFLUX], sem)
        copy.start()
        copy.wait()


def shards(
    checkpoint,
    adjoint_in,
    land_mask,
    diffusivity,
    penetration,
    column_weight,
    routes,
    dest_row,
    weight_id,
    regrid_table,
):
    comp, lat, lon = lax.axis_index("comp"), lax.axis_index("lat"), lax.axis_index("lon")
    place = jnp.stack([comp, lat, lon]).astype(jnp.int32)
    state, adj = checkpoint[0], adjoint_in[0]
    spread_weight = jnp.repeat(column_weight, 4, axis=1)
    own_row = iota((1, 4, PLANES * ROWS), 2) % 4 == iota((1, 4, PLANES * ROWS), 1)
    weight = jnp.where(own_row, spread_weight[:, None, :], 0.0).reshape(16, PLANES * ROWS)

    routing = jnp.concatenate(
        [routes.reshape(2, LANES), dest_row.reshape(2, LANES), weight_id.reshape(2, LANES), jnp.zeros((2, LANES), jnp.int32)]
    )
    edge = jax.ShapeDtypeStruct((2 * PLANES + 1, 8, COLS), f32)
    flux, to_north, to_south = pl.pallas_call(
        flux_kernel,
        out_shape=(jax.ShapeDtypeStruct((32, LANES), f32), edge, edge),
        in_specs=[smem()] + [vmem()] * 4,
        out_specs=(vmem(),) * 3,
        compiler_params=pltpu.CompilerParams(vmem_limit_bytes=12 << 20),
        name="flux",
    )(place, state, adj, land_mask, weight)
    sent = [lax.ppermute(flux, "comp", [(3, band)]) for band in range(3)]
    from_south = lax.ppermute(to_north, "lat", [(i, i + 1) for i in range(3)])
    from_north = lax.ppermute(to_south, "lat", [(i + 1, i) for i in range(3)])
    routing_all = lax.all_to_all(
        jnp.broadcast_to(routing[None], (TILES, 8, LANES)), ("lat", "lon"), split_axis=0, concat_axis=0, tiled=True
    ).reshape(TILES * 8, LANES)

    strip = jax.ShapeDtypeStruct((2, HALO_ROWS, LANES), f32)
    to_east, to_west = pl.pallas_call(
        strip_kernel,
        out_shape=(strip, strip),
        in_specs=[vmem()] * 5,
        out_specs=(vmem(),) * 2,
        compiler_params=pltpu.CompilerParams(vmem_limit_bytes=12 << 20),
        name="strips",
    )(state, adj, land_mask, from_south, from_north)
    from_west = lax.ppermute(to_east, "lon", [(i, (i + 1) % 16) for i in range(16)])
    from_east = lax.ppermute(to_west, "lon", [((i + 1) % 16, i) for i in range(16)])

    here = jnp.where(comp == 3, flux, sent[0] + sent[1] + sent[2])
    flux_all = lax.all_to_all(
        jnp.broadcast_to(here[None], (TILES, 32, LANES)), ("lat", "lon"), split_axis=0, concat_axis=0, tiled=True
    ).reshape(TILES * 32, LANES)

    high, low, spread_own, spread_side = pl.pallas_call(
        route_kernel,
        out_shape=(
            in_vmem((12 * ADJ_ROWS, 1024), bf16),
            in_vmem((12 * ADJ_ROWS, 1024), bf16),
            in_vmem((512, 512), bf16),
            in_vmem((512, 256), bf16),
        ),
        in_specs=[smem(), smem(), vmem()],
        out_specs=(vmem(),) * 4,
        scratch_shapes=[
            VM((3, LANES, LANES), f32),
            VM((4, LANES, LANES), f32),
            VM((8, 12, ADJ_ROWS, LANES), f32),
        ],
        compiler_params=pltpu.CompilerParams(vmem_limit_bytes=16 << 20),
        name="routing",
    )(place, regrid_table, routing_all)

    wide = (ADJ_ROWS, WIDE)
    prepared = pl.pallas_call(
        forward_kernel,
        out_shape=(
            in_vmem(wide),
            in_vmem((NFLUX, LEVB) + wide),
            in_vmem((NSTEP, LEVB) + wide),
            in_vmem((NSTEP, LEVB) + wide),
            in_vmem((NSTEP, NFLUX, LEVB) + wide),
            in_vmem((NSTEP, NFLUX, LEVB) + wide),
            in_vmem((NSTEP, LEVB) + wide),
            in_vmem((NSTEP, LEVB) + wide),
            jax.ShapeDtypeStruct((FLD, LEVB, ROWS, COLS), f32),
        ),
        in_specs=[smem(), smem()] + [vmem()] * 7,
        out_specs=(vmem(),) * 9,
        scratch_shapes=[
            VM((2, PLANES, HALO_ROWS, WIDE), f32),
            VM((HALO_ROWS, WIDE), f32),
            VM((FLD - NFLUX, LEVB) + wide, f32),
            VM((NSTEP, FLD - NFLUX, LEVB) + wide, f32),
            VM((NSTEP, FLD - NFLUX, LEVB) + wide, f32),
        ],
        compiler_params=pltpu.CompilerParams(vmem_limit_bytes=32 << 20),
        name="forward",
    )(place, diffusivity, state, adj, land_mask, from_south, from_north, from_west, from_east)
    base = prepared[8]

    result = pl.pallas_call(
        adjoint_kernel,
        out_shape=jax.ShapeDtypeStruct((FLD, LEVB, ROWS, COLS), f32),
        in_specs=[smem()] * 3 + [vmem()] * 13 + [pl.BlockSpec(memory_space=pl.ANY)],
        out_specs=pl.BlockSpec(memory_space=pl.ANY),
        scratch_shapes=[
            VM((1024, COLS), bf16),
            VM((1024, COLS), bf16),
            VM((NFLUX, LEVB) + wide, f32),
            VM((NFLUX, LEVB, ROWS, COLS), f32),
            pltpu.SemaphoreType.DMA,
        ],
        input_output_aliases={16: 0},
        compiler_params=pltpu.CompilerParams(vmem_limit_bytes=32 << 20),
        name="adjoint",
    )(place, diffusivity, penetration, flux_all, high, low, spread_own, spread_side, *prepared[:8], base)
    return result[None]


def solution(mesh):
    in_specs = (
        P("comp", None, None, "lat", "lon"),
        P("comp", None, None, "lat", "lon"),
        P("lat", "lon"),
        P(),
        P(),
        P(),
        P(("lat", "lon"), None),
        P(("lat", "lon")),
        P(("lat", "lon")),
        P(),
    )
    out_specs = P("comp", None, None, "lat", "lon")
    return jax.shard_map(shards, mesh=mesh, in_specs=in_specs, out_specs=out_specs, check_vma=False)
```

profile of v0, /device:TPU:1, one launch (start us, length us, event | category | flops | bytes accessed | tf_op | source)
XLA Modules:
  0.0 117.9 jit_solution(16273065288983555956)
XLA Ops:
  0.1 0.9 add_add_fusion
  1.0 0.7 broadcast_in_dim.50
  1.7 10.3 %all-to-all-start.1 = ((s32[64,8,128]{2,1,0:T(8,128)}), s32[64,8,128]{2,1,0:T(8,128)S(1)}, u32[]{:S(2)}, u32[]{:S(2)}) async-start(s32[64,8,128]{2,1,0:T(8,128)} %broadcast_in_dim.50), calls=%async_computation.1 | async-start | bytes 524288 | tf_op jit(solution)/shard_map/all_to_all | solution.py:421
  12.1 0.8 broadcast_in_dim.44
  13.3 1.1 copy-done
  14.5 1.1 copy-done.2
  15.6 0.8 copy-done.22
  16.4 1.3 %flux.1 = (f32[32,128]{1,0:T(8,128)S(1)}, f32[25,8,256]{2,1,0:T(8,128)}, f32[25,8,256]{2,1,0:T(8,128)S(1)}) custom-call(s32[3]{0:T(128)S(1)} %pad_add_fusion.place, f32[6,2,64,256]{3,2,1,0:T(8,128)S(1)} %bitcast.11, f32[6,2,64,256]{3,2,1,0:T(8,128)S(1)} %bitcast.14, s32[64,256]{1,0:T(8,128)S(1)} %copy-done.22, f32[16,768]{1,0:T(8,128)S(1)} %select_n.31.weight), custom_call_target="tpu_custom_call" | custom-call | tf_op jit(solution)/shard_map/flux/pallas_call | solution.py:410
  17.7 0.7 collective-permute-start.2
  18.4 0.7 collective-permute-start.1
  19.0 1.3 %collective-permute-start = (f32[32,128]{1,0:T(8,128)S(1)}, f32[32,128]{1,0:T(8,128)S(1)}, u32[]{:S(2)}, u32[]{:S(2)}) collective-permute-start(f32[32,128]{1,0:T(8,128)S(1)} %get-tuple-element.23), channel_id=1, source_target_pairs={{192,0},{193,1},{194,2},{195,3},{196,4},{197,5},{198,6},{199,7},{2... | collective-permute-start | bytes 49160 | tf_op jit(solution)/shard_map/ppermute | solution.py:418
  20.4 9.2 %collective-permute-done = f32[32,128]{1,0:T(8,128)S(1)} collective-permute-done((f32[32,128]{1,0:T(8,128)S(1)}, f32[32,128]{1,0:T(8,128)S(1)}, u32[]{:S(2)}, u32[]{:S(2)}) %collective-permute-start) | collective-permute-done | bytes 16416 | tf_op jit(solution)/shard_map/ppermute | solution.py:418
  29.6 1.1 broadcast_in_dim.48
  30.7 10.1 %all-to-all-start = ((f32[64,32,128]{2,1,0:T(8,128)}), f32[64,32,128]{2,1,0:T(8,128)S(1)}, u32[]{:S(2)}, u32[]{:S(2)}) async-start(f32[64,32,128]{2,1,0:T(8,128)} %broadcast_in_dim.48), calls=%async_computation | async-start | bytes 2097152 | tf_op jit(solution)/shard_map/all_to_all | solution.py:438
  40.8 3.3 %collective-permute-start.3 = (f32[25,8,256]{2,1,0:T(8,128)}, f32[25,8,256]{2,1,0:T(8,128)S(1)}, u32[]{:S(2)}, u32[]{:S(2)}) collective-permute-start(f32[25,8,256]{2,1,0:T(8,128)} %get-tuple-element.28), channel_id=1, source_target_pairs={{0,16},{16,32},{32,48},{1,17},{17,33},{33,49},{2,18},{18,34},{34,5... | collective-permute-start | bytes 614408 | tf_op jit(solution)/shard_map/ppermute | solution.py:419
  44.2 1.3 %collective-permute-start.4 = (f32[25,8,256]{2,1,0:T(8,128)}, f32[25,8,256]{2,1,0:T(8,128)S(1)}, u32[]{:S(2)}, u32[]{:S(2)}) collective-permute-start(f32[25,8,256]{2,1,0:T(8,128)} %copy-done.32), channel_id=1, source_target_pairs={{16,0},{32,16},{48,32},{17,1},{33,17},{49,33},{18,2},{34,18},{50,3... | collective-permute-start | bytes 614408 | tf_op jit(solution)/shard_map/ppermute | solution.py:420
  45.5 11.0 %collective-permute-done.3.from_south = f32[25,8,256]{2,1,0:T(8,128)S(1)} collective-permute-done((f32[25,8,256]{2,1,0:T(8,128)}, f32[25,8,256]{2,1,0:T(8,128)S(1)}, u32[]{:S(2)}, u32[]{:S(2)}) %collective-permute-start.3) | collective-permute-done | bytes 204832 | tf_op jit(solution)/shard_map/ppermute | solution.py:419
  56.5 2.0 %collective-permute-done.4.from_north = f32[25,8,256]{2,1,0:T(8,128)S(1)} collective-permute-done((f32[25,8,256]{2,1,0:T(8,128)}, f32[25,8,256]{2,1,0:T(8,128)S(1)}, u32[]{:S(2)}, u32[]{:S(2)}) %collective-permute-start.4) | collective-permute-done | bytes 204832 | tf_op jit(solution)/shard_map/ppermute | solution.py:420
  58.5 1.2 %strips.1 = (f32[2,80,128]{2,1,0:T(8,128)}, f32[2,80,128]{2,1,0:T(8,128)}) custom-call(f32[6,2,64,256]{3,2,1,0:T(8,128)S(1)} %bitcast.12, f32[6,2,64,256]{3,2,1,0:T(8,128)S(1)} %bitcast.15, s32[64,256]{1,0:T(8,128)S(1)} %copy-done.23, f32[25,8,256]{2,1,0:T(8,128)S(1)} %collective-permute-done.3.from_south, f32[25,8,256]{2,1,0:T(8,128)S(1)} %collective-permute-done.4.from_north), custom_call_target="tpu_custom_call" | custom-call | tf_op jit(solution)/shard_map/strips/pallas_call | solution.py:426
  59.7 1.9 %collective-permute-start.5 = (f32[2,80,128]{2,1,0:T(8,128)}, f32[2,80,128]{2,1,0:T(8,128)S(1)}, u32[]{:S(2)}, u32[]{:S(2)}) collective-permute-start(f32[2,80,128]{2,1,0:T(8,128)} %get-tuple-element.30), channel_id=1, source_target_pairs={{0,1},{1,2},{2,3},{3,4},{4,5},{5,6},{6,7},{7,8},{8,9},{9,10},{10,1... | collective-permute-start | bytes 245768 | tf_op jit(solution)/shard_map/ppermute | solution.py:434
  61.7 0.8 copy.13.table
  62.4 1.0 collective-permute-done.5.from_west
  63.5 2.6 %collective-permute-done.6.from_east = f32[2,80,128]{2,1,0:T(8,128)S(1)} collective-permute-done((f32[2,80,128]{2,1,0:T(8,128)}, f32[2,80,128]{2,1,0:T(8,128)S(1)}, u32[]{:S(2)}, u32[]{:S(2)}) %collective-permute-start.6) | collective-permute-done | bytes 81952 | tf_op jit(solution)/shard_map/ppermute | solution.py:435
  66.7 0.9 copy-done.25
  68.1 0.7 copy-done.29
  68.8 8.4 %forward.1 = (f32[72,384]{1,0:T(8,128)S(1)}, f32[4,2,72,384]{3,2,1,0:T(8,128)S(1)}, f32[4,2,72,384]{3,2,1,0:T(8,128)S(1)}, f32[4,2,72,384]{3,2,1,0:T(8,128)S(1)}...) custom-call(s32[3]{0:T(128)S(1)} %copy-done.27, ...), custom_call_target="tpu_custom_call" | custom-call | tf_op jit(solution)/shard_map/forward/pallas_call | solution.py:462
  77.2 1.7 %copy-done.4 = f32[4,4,2,72,384]{4,3,2,1,0:T(8,128)} copy-done((f32[4,4,2,72,384]{4,3,2,1,0:T(8,128)}, f32[4,4,2,72,384]{4,3,2,1,0:T(8,128)S(1)}, u32[]{:S(2)}) %copy-start.4) | copy-done | bytes 3538968
  78.9 1.8 %copy-done.6 = f32[4,4,2,72,384]{4,3,2,1,0:T(8,128)} copy-done((f32[4,4,2,72,384]{4,3,2,1,0:T(8,128)}, f32[4,4,2,72,384]{4,3,2,1,0:T(8,128)S(1)}, u32[]{:S(2)}) %copy-start.6) | copy-done | bytes 3538968
  80.7 1.0 copy-done.12
  81.7 0.9 copy-done.14
  82.6 0.9 copy-done.16
  83.5 0.9 copy-done.18
  84.4 0.9 copy-done.20
  85.4 7.7 %routing.1 = (bf16[864,1024]{1,0:T(8,128)(2,1)S(1)}, bf16[864,1024]{1,0:T(8,128)(2,1)S(1)}, bf16[512,512]{1,0:T(8,128)(2,1)S(1)}, bf16[512,256]{1,0:T(8,128)(2,1)S(1)}) custom-call(s32[3]{0:T(128)S(1)} %copy-done.27, f32[8,4]{1,0:T(8,128)S(1)} %copy.13.table, s32[512,128]{1,0:T(8,128)S(1)} %bitcast.18), custom_call_target="tpu_custom_call" | custom-call | tf_op jit(solution)/shard_map/routing/pallas_call | solution.py:442
  93.1 1.3 %copy-done.8 = bf16[864,1024]{1,0:T(8,128)(2,1)} copy-done((bf16[864,1024]{1,0:T(8,128)(2,1)}, bf16[864,1024]{1,0:T(8,128)(2,1)S(1)}, u32[]{:S(2)}) %copy-start.8) | copy-done | bytes 1769496
  94.4 1.2 %copy-done.10 = bf16[864,1024]{1,0:T(8,128)(2,1)} copy-done((bf16[864,1024]{1,0:T(8,128)(2,1)}, bf16[864,1024]{1,0:T(8,128)(2,1)S(1)}, u32[]{:S(2)}) %copy-start.10) | copy-done | bytes 1769496
  95.6 2.0 %copy-done.5 = f32[4,4,2,72,384]{4,3,2,1,0:T(8,128)S(1)} copy-done((f32[4,4,2,72,384]{4,3,2,1,0:T(8,128)S(1)}, f32[4,4,2,72,384]{4,3,2,1,0:T(8,128)}, u32[]{:S(2)}) %copy-start.5) | copy-done | bytes 3538968
  97.6 2.0 %copy-done.7 = f32[4,4,2,72,384]{4,3,2,1,0:T(8,128)S(1)} copy-done((f32[4,4,2,72,384]{4,3,2,1,0:T(8,128)S(1)}, f32[4,4,2,72,384]{4,3,2,1,0:T(8,128)}, u32[]{:S(2)}) %copy-start.7) | copy-done | bytes 3538968
  99.6 1.5 %copy-done.9 = bf16[864,1024]{1,0:T(8,128)(2,1)S(1)} copy-done((bf16[864,1024]{1,0:T(8,128)(2,1)S(1)}, bf16[864,1024]{1,0:T(8,128)(2,1)}, u32[]{:S(2)}) %copy-start.9) | copy-done | bytes 1769496
  101.1 1.5 %copy-done.11 = bf16[864,1024]{1,0:T(8,128)(2,1)S(1)} copy-done((bf16[864,1024]{1,0:T(8,128)(2,1)S(1)}, bf16[864,1024]{1,0:T(8,128)(2,1)}, u32[]{:S(2)}) %copy-start.11) | copy-done | bytes 1769496
  102.6 1.2 copy-done.13
  103.7 1.2 copy-done.15
  104.9 1.2 copy-done.17
  106.1 1.2 copy-done.19
  107.2 1.2 copy-done.21
  109.0 0.7 copy-done.30
  109.6 0.7 copy-done.31
  110.3 7.5 %adjoint.1 = f32[6,2,64,256]{3,2,1,0:T(8,128)} custom-call(s32[3]{0:T(128)S(1)} %copy-done.28, f32[6]{0:T(128)S(1)} %copy-done.30, f32[6]{0:T(128)S(1)} %copy-done.31, f32[2048,128]{1,0:T(8,128)S(1)} %bitcast.17, bf16[864,1024]{1,0:T(8,128)(2,1)S(1)} %copy-done.9, bf16[864,1024]{1,0:T(8,128)(2,1)S(1)} %copy-done.11, ...), custom_call_target="tpu_custom_call", output_to_operand_aliasing={{}: (16, {})} | custom-call | tf_op jit(solution)/shard_map/adjoint/pallas_call | solution.py:489
  (56 shorter events, 2.4 us)
Async XLA Ops:
  0.0 58.5 %copy-start.23 = (s32[64,256]{1,0:T(8,128)S(1)}, s32[64,256]{1,0:T(8,128)}, u32[]{:S(2)}) copy-start(s32[64,256]{1,0:T(8,128)} %mask.5) | copy-start | bytes 196612
  0.0 58.5 %copy-start.3 = (f32[1,6,2,64,256]{4,3,2,1,0:T(8,128)S(1)}, f32[1,6,2,64,256]{4,3,2,1,0:T(8,128)}, u32[]{:S(2)}) copy-start(f32[1,6,2,64,256]{4,3,2,1,0:T(8,128)} %param.11) | copy-start | bytes 2359300
  0.0 58.5 %copy-start.1 = (f32[1,6,2,64,256]{4,3,2,1,0:T(8,128)S(1)}, f32[1,6,2,64,256]{4,3,2,1,0:T(8,128)}, u32[]{:S(2)}) copy-start(f32[1,6,2,64,256]{4,3,2,1,0:T(8,128)} %param.10) | copy-start | bytes 2359300
  1.7 27.9 %all-to-all-start.1 = ((s32[64,8,128]{2,1,0:T(8,128)}), s32[64,8,128]{2,1,0:T(8,128)S(1)}, u32[]{:S(2)}, u32[]{:S(2)}) async-start(s32[64,8,128]{2,1,0:T(8,128)} %broadcast_in_dim.50), calls=%async_computation.1 | async-start | bytes 524288 | tf_op jit(solution)/shard_map/all_to_all | solution.py:421
  13.3 5.0 %copy-start.26 = (s32[3]{0:T(128)}, s32[3]{0:T(128)S(1)}, u32[]{:S(2)}) copy-start(s32[3]{0:T(128)S(1)} %pad_add_fusion.place) | copy-start | bytes 40
  13.3 1.1 copy-start
  14.5 1.1 copy-start.2
  15.6 0.8 copy-start.22
  17.7 23.1 %copy-start.32 = (f32[25,8,256]{2,1,0:T(8,128)}, f32[25,8,256]{2,1,0:T(8,128)S(1)}, u32[]{:S(2)}) copy-start(f32[25,8,256]{2,1,0:T(8,128)S(1)} %get-tuple-element.29) | copy-start | bytes 614404
  17.7 2.6 %collective-permute-start.2 = (f32[32,128]{1,0:T(8,128)S(1)}, f32[32,128]{1,0:T(8,128)S(1)}, u32[]{:S(2)}, u32[]{:S(2)}) collective-permute-start(f32[32,128]{1,0:T(8,128)S(1)} %get-tuple-element.23), channel_id=1, source_target_pairs={{192,128},{193,129},{194,130},{195,131},{196,132},{197,133},{198,1... | collective-permute-start | bytes 49160 | tf_op jit(solution)/shard_map/ppermute | solution.py:418
  18.4 2.0 %collective-permute-start.1 = (f32[32,128]{1,0:T(8,128)S(1)}, f32[32,128]{1,0:T(8,128)S(1)}, u32[]{:S(2)}, u32[]{:S(2)}) collective-permute-start(f32[32,128]{1,0:T(8,128)S(1)} %get-tuple-element.23), channel_id=1, source_target_pairs={{192,64},{193,65},{194,66},{195,67},{196,68},{197,69},{198,70},{19... | collective-permute-start | bytes 49160 | tf_op jit(solution)/shard_map/ppermute | solution.py:418
  19.0 10.6 %collective-permute-start = (f32[32,128]{1,0:T(8,128)S(1)}, f32[32,128]{1,0:T(8,128)S(1)}, u32[]{:S(2)}, u32[]{:S(2)}) collective-permute-start(f32[32,128]{1,0:T(8,128)S(1)} %get-tuple-element.23), channel_id=1, source_target_pairs={{192,0},{193,1},{194,2},{195,3},{196,4},{197,5},{198,6},{199,7},{2... | collective-permute-start | bytes 49160 | tf_op jit(solution)/shard_map/ppermute | solution.py:418
  30.7 64.9 %all-to-all-start = ((f32[64,32,128]{2,1,0:T(8,128)}), f32[64,32,128]{2,1,0:T(8,128)S(1)}, u32[]{:S(2)}, u32[]{:S(2)}) async-start(f32[64,32,128]{2,1,0:T(8,128)} %broadcast_in_dim.48), calls=%async_computation | async-start | bytes 2097152 | tf_op jit(solution)/shard_map/all_to_all | solution.py:438
  40.8 15.6 %collective-permute-start.3 = (f32[25,8,256]{2,1,0:T(8,128)}, f32[25,8,256]{2,1,0:T(8,128)S(1)}, u32[]{:S(2)}, u32[]{:S(2)}) collective-permute-start(f32[25,8,256]{2,1,0:T(8,128)} %get-tuple-element.28), channel_id=1, source_target_pairs={{0,16},{16,32},{32,48},{1,17},{17,33},{33,49},{2,18},{18,34},{34,5... | collective-permute-start | bytes 614408 | tf_op jit(solution)/shard_map/ppermute | solution.py:419
  44.2 14.3 %collective-permute-start.4 = (f32[25,8,256]{2,1,0:T(8,128)}, f32[25,8,256]{2,1,0:T(8,128)S(1)}, u32[]{:S(2)}, u32[]{:S(2)}) collective-permute-start(f32[25,8,256]{2,1,0:T(8,128)} %copy-done.32), channel_id=1, source_target_pairs={{16,0},{32,16},{48,32},{17,1},{33,17},{49,33},{18,2},{34,18},{50,3... | collective-permute-start | bytes 614408 | tf_op jit(solution)/shard_map/ppermute | solution.py:420
  59.7 3.7 %collective-permute-start.5 = (f32[2,80,128]{2,1,0:T(8,128)}, f32[2,80,128]{2,1,0:T(8,128)S(1)}, u32[]{:S(2)}, u32[]{:S(2)}) collective-permute-start(f32[2,80,128]{2,1,0:T(8,128)} %get-tuple-element.30), channel_id=1, source_target_pairs={{0,1},{1,2},{2,3},{3,4},{4,5},{5,6},{6,7},{7,8},{8,9},{9,10},{10,1... | collective-permute-start | bytes 245768 | tf_op jit(solution)/shard_map/ppermute | solution.py:434
  61.6 4.4 %collective-permute-start.6 = (f32[2,80,128]{2,1,0:T(8,128)}, f32[2,80,128]{2,1,0:T(8,128)S(1)}, u32[]{:S(2)}, u32[]{:S(2)}) collective-permute-start(f32[2,80,128]{2,1,0:T(8,128)} %get-tuple-element.31), channel_id=1, source_target_pairs={{1,0},{2,1},{3,2},{4,3},{5,4},{6,5},{7,6},{8,7},{9,8},{10,9},{11,1... | collective-permute-start | bytes 245768 | tf_op jit(solution)/shard_map/ppermute | solution.py:435
  66.0 0.6 copy-start.24
  66.7 0.9 copy-start.25
  67.5 0.6 copy-start.27
  68.1 0.7 copy-start.29
  77.2 1.7 %copy-start.4 = (f32[4,4,2,72,384]{4,3,2,1,0:T(8,128)}, f32[4,4,2,72,384]{4,3,2,1,0:T(8,128)S(1)}, u32[]{:S(2)}) copy-start(f32[4,4,2,72,384]{4,3,2,1,0:T(8,128)S(1)} %get-tuple-element.36.grad_e) | copy-start | bytes 10616836
  78.9 1.8 %copy-start.6 = (f32[4,4,2,72,384]{4,3,2,1,0:T(8,128)}, f32[4,4,2,72,384]{4,3,2,1,0:T(8,128)S(1)}, u32[]{:S(2)}) copy-start(f32[4,4,2,72,384]{4,3,2,1,0:T(8,128)S(1)} %get-tuple-element.37.grad_n) | copy-start | bytes 10616836
  80.7 1.0 copy-start.12
  81.7 0.9 copy-start.14
  82.6 0.9 copy-start.16
  83.5 0.9 copy-start.18
  84.4 0.9 copy-start.20
  93.1 1.3 %copy-start.8 = (bf16[864,1024]{1,0:T(8,128)(2,1)}, bf16[864,1024]{1,0:T(8,128)(2,1)S(1)}, u32[]{:S(2)}) copy-start(bf16[864,1024]{1,0:T(8,128)(2,1)S(1)} %get-tuple-element.24.high) | copy-start | bytes 5308420
  94.4 1.2 %copy-start.10 = (bf16[864,1024]{1,0:T(8,128)(2,1)}, bf16[864,1024]{1,0:T(8,128)(2,1)S(1)}, u32[]{:S(2)}) copy-start(bf16[864,1024]{1,0:T(8,128)(2,1)S(1)} %get-tuple-element.25.low) | copy-start | bytes 5308420
  95.6 2.0 %copy-start.5 = (f32[4,4,2,72,384]{4,3,2,1,0:T(8,128)S(1)}, f32[4,4,2,72,384]{4,3,2,1,0:T(8,128)}, u32[]{:S(2)}) copy-start(f32[4,4,2,72,384]{4,3,2,1,0:T(8,128)} %copy-done.4) | copy-start | bytes 10616836
  97.6 2.0 %copy-start.7 = (f32[4,4,2,72,384]{4,3,2,1,0:T(8,128)S(1)}, f32[4,4,2,72,384]{4,3,2,1,0:T(8,128)}, u32[]{:S(2)}) copy-start(f32[4,4,2,72,384]{4,3,2,1,0:T(8,128)} %copy-done.6) | copy-start | bytes 10616836
  99.6 1.5 %copy-start.9 = (bf16[864,1024]{1,0:T(8,128)(2,1)S(1)}, bf16[864,1024]{1,0:T(8,128)(2,1)}, u32[]{:S(2)}) copy-start(bf16[864,1024]{1,0:T(8,128)(2,1)} %copy-done.8) | copy-start | bytes 5308420
  101.1 1.5 %copy-start.11 = (bf16[864,1024]{1,0:T(8,128)(2,1)S(1)}, bf16[864,1024]{1,0:T(8,128)(2,1)}, u32[]{:S(2)}) copy-start(bf16[864,1024]{1,0:T(8,128)(2,1)} %copy-done.10) | copy-start | bytes 5308420
  102.6 1.2 copy-start.13
  103.7 1.2 copy-start.15
  104.9 1.2 copy-start.17
  106.1 1.2 copy-start.19
  107.2 1.2 copy-start.21
  108.4 0.6 copy-start.28
  109.0 0.7 copy-start.30
  109.6 0.7 copy-start.31
where the time goes:
time: 120 us; the launch traced here: 118 us
  local copies, waits for them, and re-layouts  35 us (29%)
  starting transfers between devices  29.6 us (25%)
  Pallas kernels  26.1 us (22%)
  waiting for transfers between devices  25.9 us (22%)
    unnamed x67, local copies, waits for them, and re-layouts  32 us
    ppermute x1, waiting for transfers between devices, shards(): from_south = lax.ppermute(to_north, 'lat', [(i, i + 1) for i in range(3)])  11 us
    all_to_all x1, starting transfers between devices, shards(): lax.all_to_all(jnp.broadcast_to(routing[None], (TILES, 8, LANES)), ('lat'...  10.3 us
    all_to_all x1, starting transfers between devices, shards(): lax.all_to_all(jnp.broadcast_to(here[None], (TILES, 32, LANES)), ('lat',...  10.1 us
    ppermute x3, waiting for transfers between devices, shards(): sent = [lax.ppermute(flux, 'comp', [(3, band)]) for band in range(3)]  9.25 us
    pallas_call x1, Pallas kernels, shards(): pl.pallas_call(forward_kernel, out_shape=(in_vmem(wide), in_vmem((NFLUX,...  8.37 us
    pallas_call x1, Pallas kernels, shards(): pl.pallas_call(route_kernel, out_shape=(in_vmem((12 * ADJ_ROWS, 1024), bf...  7.71 us
    pallas_call x1, Pallas kernels, shards(): pl.pallas_call(adjoint_kernel, out_shape=jax.ShapeDtypeStruct((FLD, LEVB,...  7.48 us
  transfers between devices with their start and end apart: 9, of which 5 were waited for; matrix products, arithmetic and copies ran while one was open for 2% of the time, Pallas kernels for 16%

commit v1 on v0

v1 whole, which is shorter than its diff:
```python
import jax
import jax.numpy as jnp
import ml_dtypes
import numpy as np
from jax import lax
from jax.experimental import pallas as pl
from jax.experimental.pallas import tpu as pltpu
from jax.sharding import PartitionSpec as P

NSTEP = 4
STEP_COEF = 0.2
SPEED_BASE = 0.5
SPEED_GAIN = 0.5

FLD = 6
NFLUX = 4
LEVB = 2
ROWS = 64
COLS = 256
PLANES = FLD * LEVB
HALO_ROWS = 80
ADJ_ROWS = 72
WIDE = 384
LANES = 128
TILES = 64
SEGS = 16
FAR = -1.0

f32 = jnp.float32
bf16 = jnp.bfloat16
VM = pltpu.VMEM
SM = pltpu.SMEM


def vmem():
    return pl.BlockSpec(memory_space=VM)


def smem():
    return pl.BlockSpec(memory_space=SM)


def in_hbm():
    return pl.BlockSpec(memory_space=pltpu.HBM)


def hbm(x):
    return pltpu.with_memory_space_constraint(jnp.asarray(x), pltpu.HBM)


def shape_of(shape, dtype=f32):
    return jax.ShapeDtypeStruct(shape, dtype)


def east(x):
    return pltpu.roll(x, WIDE - 1, 1)


def west(x):
    return pltpu.roll(x, 1, 1)


def north(x):
    return pltpu.roll(x, x.shape[0] - 1, 0)


def south(x):
    return pltpu.roll(x, 1, 0)


def iota(shape, dim):
    return lax.broadcasted_iota(jnp.int32, shape, dim)


def split(x):
    high = x.astype(bf16)
    return high, (x - high.astype(f32)).astype(bf16)


def dot(x, y):
    return jnp.dot(x, y, preferred_element_type=f32)


def flux_kernel(
    checkpoint, adjoint_in, mask, weight, flux, to_north, to_south, held, held_adj, held_mask, held_weight, sems
):
    copies = [
        pltpu.make_async_copy(source, target, sems.at[at])
        for at, (source, target) in enumerate(
            ((checkpoint, held), (adjoint_in, held_adj), (mask, held_mask), (weight, held_weight))
        )
    ]
    for copy in copies:
        copy.start()
    copies[3].wait()
    atmosphere = lax.axis_index("comp") == 3

    @pl.when(atmosphere)
    def _():
        w = held_weight[...]
        head = w.astype(bf16).astype(f32)
        rest = w - head
        middle = rest.astype(bf16).astype(f32)
        parts = jnp.concatenate([head, middle, rest - middle, jnp.zeros_like(w)], axis=0).astype(bf16)
        level, row = iota((FLD * 32, PLANES * ROWS), 0), iota((FLD * 32, PLANES * ROWS), 1)
        repeated = dot(parts, jnp.where(row // 4 == level, 1.0, 0.0).astype(bf16))
        repeated = repeated[0:4] + repeated[4:8] + repeated[8:12]
        own = iota((4, PLANES * ROWS), 1) % 4 == iota((4, PLANES * ROWS), 0)
        spread = jnp.concatenate([jnp.where(own, repeated[k : k + 1], 0.0) for k in range(NFLUX)], axis=0)
        for copy in copies[:3]:
            copy.wait()
        t = jnp.tanh(held[...])
        sens = (held_adj[...] * (1.0 - t * t)).reshape(PLANES * ROWS, COLS)
        by_kind = jnp.dot(spread, sens, precision=lax.Precision.HIGHEST, preferred_element_type=f32)
        rows = []
        for q in range(4):
            rows.append(
                jnp.concatenate(
                    [by_kind[k * 4 : k * 4 + 4, q * 64 : q * 64 + 64] for k in range(NFLUX)], axis=1
                )
            )
        by_seg = jnp.concatenate(rows, axis=0)
        flux[0:16, :] = by_seg[:, 0:LANES]
        flux[16:32, :] = by_seg[:, LANES:]

    @pl.when(jnp.logical_not(atmosphere))
    def _():
        flux[...] = jnp.zeros((32, LANES), f32)
        for copy in copies[:3]:
            copy.wait()
        for plane in range(PLANES):
            f, l = plane // LEVB, plane % LEVB
            to_north[plane] = held[f, l, ROWS - 8 : ROWS, :]
            to_south[plane] = held[f, l, 0:8, :]
            to_north[PLANES + plane] = held_adj[f, l, ROWS - 8 : ROWS, :]
            to_south[PLANES + plane] = held_adj[f, l, 0:8, :]
        to_north[2 * PLANES] = held_mask[ROWS - 8 : ROWS, :].astype(f32)
        to_south[2 * PLANES] = held_mask[0:8, :].astype(f32)


def payload_kernel(flux, first, second, third, routes, dest_row, weight_id, from_south, from_north, payload):
    del from_south, from_north
    whole = flux[...] + (first[...] + second[...] + third[...])
    listing = [x[...].astype(f32) for x in (routes, dest_row, weight_id)]
    listing = jnp.concatenate(listing + [jnp.zeros((2, LANES), f32)], axis=0)

    def copy_out(tile, carry):
        payload[tile, 0:32, :] = whole
        payload[tile, 32:40, :] = listing
        return carry

    lax.fori_loop(0, TILES, copy_out, 0)


def strip_kernel(checkpoint, adjoint_in, mask, from_south, from_north, to_east, to_west):
    lane_group = iota((HALO_ROWS, LANES), 1) // 8
    for kind, source in enumerate((checkpoint, adjoint_in)):
        east_strip = jnp.zeros((HALO_ROWS, LANES), f32)
        west_strip = jnp.zeros((HALO_ROWS, LANES), f32)
        for plane in range(PLANES + 1 - kind):
            if plane < PLANES:
                f, l = plane // LEVB, plane % LEVB
                at = kind * PLANES + plane
                own_w, own_e = source[f, l, :, 0:LANES], source[f, l, :, LANES:]
            else:
                at = 2 * PLANES
                own_w, own_e = mask[:, 0:LANES].astype(f32), mask[:, LANES:].astype(f32)
            edge_w = jnp.concatenate([own_w, from_north[at, :, 0:LANES], from_south[at, :, 0:LANES]], axis=0)
            edge_e = jnp.concatenate([own_e, from_north[at, :, LANES:], from_south[at, :, LANES:]], axis=0)
            east_strip = jnp.where(lane_group == plane, pltpu.roll(edge_e, 8 * plane + 8, 1), east_strip)
            moved = edge_w if plane == 0 else pltpu.roll(edge_w, 8 * plane, 1)
            west_strip = jnp.where(lane_group == plane, moved, west_strip)
        to_east[kind] = east_strip
        to_west[kind] = west_strip


def to_adjoint_rows(x):
    row = iota((8, WIDE), 0)
    return jnp.concatenate([x[0:ROWS], jnp.where(row < 4, x[ROWS : ROWS + 8], x[ROWS + 8 :])], axis=0)


def pulled(mu, a, b, d):
    mixed, carried_e, carried_n = d * mu, a * mu, b * mu
    return (
        (1.0 - 4.0 * d) * mu
        + (east(mixed + carried_e) + west(mixed - carried_e))
        + (north(mixed + carried_n) + south(mixed - carried_n))
    )


def route_matrix(gathered, table, high, low, code_t, prof_t, total):
    lat_me, lon_me = lax.axis_index("lat"), lax.axis_index("lon")

    def listed(at):
        parts = [gathered[pl.ds(32 + 2 * at + half, TILES, stride=40), :] for half in range(2)]
        return jnp.concatenate(parts, axis=0).astype(jnp.int32)

    dest, row, profile = listed(0), listed(1), listed(2)
    dest_lat, dest_lon = dest // 16, dest % 16
    row = row + ROWS * (dest_lat - lat_me)
    valid = jnp.logical_and(row >= -4, row < ROWS + 4)
    code = jnp.where(row < 0, row + ADJ_ROWS, row).astype(f32)
    for way in range(3):
        lon_of = (lon_me + (0, 1, 15)[way]) % 16
        here = jnp.logical_and(valid, dest_lon == lon_of)
        code_t[way] = jnp.where(here, code, FAR).T
    for c in range(4):
        weights = jnp.zeros((LANES, LANES), f32)
        for w in range(8):
            weights = jnp.where(profile == w, table[c, w], weights)
        prof_t[c] = weights.T
    rows = iota((ADJ_ROWS, LANES), 0).astype(f32)

    def build(step, carry):
        way, seg = step // 8, step % 8
        sums = [jnp.zeros((ADJ_ROWS, LANES), f32) for _ in range(4)]
        for r in range(16):
            at = seg * 16 + r
            hit = code_t[way, pl.ds(at, 1), :] == rows
            for c in range(4):
                sums[c] = sums[c] + jnp.where(hit, prof_t[c, pl.ds(at, 1), :], 0.0)
        for c in range(4):
            total[seg, way * 4 + c] = sums[c]
        return carry

    lax.fori_loop(0, 24, build, 0)
    for seg in range(8):
        whole = total[seg].reshape(12 * ADJ_ROWS, LANES)
        head, tail = split(whole)
        high[:, seg * LANES : (seg + 1) * LANES] = head
        low[:, seg * LANES : (seg + 1) * LANES] = tail


def spread_tables():
    src, out = np.arange(512)[:, None], np.arange(512)[None, :]
    own = ((src // 64) % 2 == out // COLS) & (out % COLS == 4 * (src % 64) + src // 128)
    out = np.arange(256)[None, :]
    first = (src % 64 == 0) & (out % LANES == src // 128)
    final = (src % 64 == 63) & (out % LANES == 124 + src // 128)
    side = ((src // 64) % 2 == out // LANES) & (first | final)
    return own.astype(ml_dtypes.bfloat16), side.astype(ml_dtypes.bfloat16)


def assemble_forcing(gathered, high, low, g_high, g_low, spread_own, spread_side):
    for seg in range(8):
        for h in range(2):
            s = h * 8 + seg
            at = (s % 4) * 4 + s // 4
            for half in range(2):
                part = gathered[pl.ds(half * 16 + at, TILES, stride=40), :]
                head, tail = split(part)
                rows = slice(seg * LANES + h * 64, seg * LANES + h * 64 + 64)
                g_high[rows, half * LANES : (half + 1) * LANES] = head
                g_low[rows, half * LANES : (half + 1) * LANES] = tail
    coarse = dot(high[...], g_high[...]) + dot(high[...], g_low[...]) + dot(low[...], g_high[...])
    own_parts, side_parts = [], []
    lane = iota((ADJ_ROWS, LANES), 1) % 64
    for half in range(2):
        cols = slice(half * LANES, (half + 1) * LANES)

        def piece(way, c):
            at = (way * 4 + c) * ADJ_ROWS
            return coarse[at : at + ADJ_ROWS, cols]

        own = jnp.concatenate([piece(0, c) for c in range(4)], axis=1)
        side = jnp.concatenate(
            [jnp.where(lane == 0, piece(1, c), jnp.where(lane == 63, piece(2, c), 0.0)) for c in range(4)], axis=1
        )
        for parts, value in ((own_parts, own), (side_parts, side)):
            head = value.astype(bf16).astype(f32)
            parts += [head, value - head]
    own = dot(jnp.concatenate(own_parts, axis=0).astype(bf16), spread_own[...])
    side = dot(jnp.concatenate(side_parts, axis=0).astype(bf16), spread_side[...])
    return own, side


def forward_steps(state, wet_all, diffusivity, speed_e, speed_n, grad_e, grad_n):
    for step in range(NSTEP):
        now, later = step % 2, (step + 1) % 2
        for l in range(LEVB):
            a = 0.5 * STEP_COEF * (SPEED_BASE + SPEED_GAIN * state[now, l])
            b = (0.5 * STEP_COEF * SPEED_GAIN) * state[now, LEVB + l]
            speed_e[step, l] = to_adjoint_rows(a)
            speed_n[step, l] = to_adjoint_rows(b)
            for f in range(FLD):
                d = diffusivity[f]
                q = state[now, f * LEVB + l]
                q_e, q_w, q_n, q_s = east(q), west(q), north(q), south(q)
                across, along = q_e - q_w, q_n - q_s
                half = -0.5 * STEP_COEF * SPEED_GAIN
                grad_e[step, f, l] = to_adjoint_rows(half * across)
                grad_n[step, f, l] = to_adjoint_rows(half * along)
                if step + 1 < NSTEP:
                    moved = (1.0 - 4.0 * d) * q + d * ((q_e + q_w) + (q_n + q_s)) - a * across - b * along
                    state[later, f * LEVB + l] = wet_all[...] * moved


def ocean_kernel(
    diffusivity_at,
    penetration_at,
    table_at,
    spread_own_at,
    spread_side_at,
    checkpoint,
    adjoint_in,
    mask,
    from_south,
    from_north,
    from_west,
    from_east,
    gathered,
    out,
    diffusivity,
    penetration,
    table,
    spread_own,
    spread_side,
    mask_own,
    state,
    lam,
    wet_all,
    wet,
    speed_e,
    speed_n,
    grad_e,
    grad_n,
    high,
    low,
    code_t,
    prof_t,
    total,
    g_high,
    g_low,
    done,
    sems,
):
    section = lax.axis_index("comp")
    pairs = [
        (diffusivity_at, diffusivity),
        (penetration_at, penetration),
        (table_at, table),
        (spread_own_at, spread_own),
        (spread_side_at, spread_side),
        (mask, mask_own),
    ]
    for plane in range(PLANES):
        f, l = plane // LEVB, plane % LEVB
        pairs.append((checkpoint.at[f, l], state.at[0, plane, 0:ROWS, 0:COLS]))
        pairs.append((adjoint_in.at[f, l], lam.at[f, l, 0:ROWS, 0:COLS]))
    copies = [pltpu.make_async_copy(source, target, sems.at[at]) for at, (source, target) in enumerate(pairs)]
    for copy in copies:
        copy.start()

    @pl.when(section == 3)
    def _():
        for copy in copies:
            copy.wait()
        for plane in range(PLANES):
            f, l = plane // LEVB, plane % LEVB
            t = jnp.tanh(state[0, plane, 0:ROWS, 0:COLS])
            done[f, l] = lam[f, l, 0:ROWS, 0:COLS] * (1.0 - t * t)

    @pl.when(section != 3)
    def _():
        for copy in copies[:3]:
            copy.wait()
        route_matrix(gathered, table, high, low, code_t, prof_t, total)
        for copy in copies[3:]:
            copy.wait()
        own, side = assemble_forcing(gathered, high, low, g_high, g_low, spread_own, spread_side)

        lane = iota((HALO_ROWS, LANES), 1)

        def edge(kind, plane):
            west_side, east_side = from_west[kind], from_east[kind]
            if plane:
                east_side = pltpu.roll(east_side, LANES - 8 * plane, 1)
            west_side = pltpu.roll(west_side, (120 - 8 * plane) % LANES, 1)
            return jnp.where(lane < 8, east_side, jnp.where(lane >= 120, west_side, 0.0))

        def rows_between(at):
            row = iota((8, COLS), 0)
            return jnp.where(row < 4, from_north[at], from_south[at])

        at = 2 * PLANES
        wet_all[0:ROWS, 0:COLS] = mask_own[...].astype(f32)
        wet_all[ROWS : ROWS + 8, 0:COLS] = from_north[at]
        wet_all[ROWS + 8 :, 0:COLS] = from_south[at]
        wet_all[:, COLS:] = edge(0, PLANES)
        wet[...] = to_adjoint_rows(wet_all[...])
        row8 = iota((8, LANES), 0)
        for f in range(FLD):
            for l in range(LEVB):
                plane = f * LEVB + l
                state[0, plane, ROWS : ROWS + 8, 0:COLS] = from_north[plane]
                state[0, plane, ROWS + 8 :, 0:COLS] = from_south[plane]
                state[0, plane, :, COLS:] = edge(0, plane)
                lam[f, l, ROWS:, 0:COLS] = rows_between(PLANES + plane)
                side_col = edge(1, plane)
                lam[f, l, 0:ROWS, COLS:] = side_col[0:ROWS]
                lam[f, l, ROWS:, COLS:] = jnp.where(row8 < 4, side_col[ROWS : ROWS + 8], side_col[ROWS + 8 :])
        w = wet[...]
        band = jnp.minimum(section, 2)
        for k in range(NFLUX):
            at, sub = (k // 2) * 2 * ADJ_ROWS, k % 2
            own_k = own[:, sub * COLS : (sub + 1) * COLS]
            side_k = side[:, sub * LANES : (sub + 1) * LANES]
            whole = jnp.concatenate(
                [x[at : at + ADJ_ROWS] + x[at + ADJ_ROWS : at + 2 * ADJ_ROWS] for x in (own_k, side_k)], axis=1
            )
            forcing = w * whole
            for l in range(LEVB):
                lam[k, l] = lam[k, l] + penetration[band * LEVB + l] * forcing

        forward_steps(state, wet_all, diffusivity, speed_e, speed_n, grad_e, grad_n)

        def back(i, carry):
            step = NSTEP - 1 - i
            for l in range(LEVB):
                a, b, w = speed_e[step, l], speed_n[step, l], wet[...]
                sum_e, sum_n = 0.0, 0.0
                for f in (2, 3, 4, 5, 1, 0):
                    mu = w * lam[f, l]
                    sum_e = sum_e + mu * grad_e[step, f, l]
                    sum_n = sum_n + mu * grad_n[step, f, l]
                    lam[f, l] = pulled(mu, a, b, diffusivity[f])
                lam[0, l] = lam[0, l] + sum_e
                lam[1, l] = lam[1, l] + sum_n
            return carry

        lax.fori_loop(0, NSTEP, back, 0)
        for f in range(FLD):
            for l in range(LEVB):
                done[f, l] = lam[f, l, 0:ROWS, 0:COLS]

    copy = pltpu.make_async_copy(done, out, sems.at[0])
    copy.start()
    copy.wait()


def shards(
    checkpoint,
    adjoint_in,
    land_mask,
    diffusivity,
    penetration,
    column_weight,
    routes,
    dest_row,
    weight_id,
    regrid_table,
):
    state, adj = checkpoint[0], adjoint_in[0]
    edge = pltpu.HBM((2 * PLANES + 1, 8, COLS), f32)
    flux, to_north, to_south = pl.pallas_call(
        flux_kernel,
        out_shape=(shape_of((32, LANES)), edge, edge),
        in_specs=[in_hbm()] * 4,
        out_specs=(vmem(),) * 3,
        scratch_shapes=[
            VM((FLD, LEVB, ROWS, COLS), f32),
            VM((FLD, LEVB, ROWS, COLS), f32),
            VM((ROWS, COLS), jnp.int32),
            VM((NFLUX, FLD * 32), f32),
            pltpu.SemaphoreType.DMA((4,)),
        ],
        compiler_params=pltpu.CompilerParams(vmem_limit_bytes=12 << 20),
        name="flux",
    )(*[hbm(x) for x in (state, adj, land_mask, column_weight)])
    sent = [lax.ppermute(flux, "comp", [(3, band)]) for band in range(3)]
    from_south = lax.ppermute(to_north, "lat", [(i, i + 1) for i in range(3)])
    from_north = lax.ppermute(to_south, "lat", [(i + 1, i) for i in range(3)])

    strip = shape_of((2, HALO_ROWS, LANES))
    to_east, to_west = pl.pallas_call(
        strip_kernel,
        out_shape=(strip, strip),
        in_specs=[vmem()] * 5,
        out_specs=(vmem(),) * 2,
        compiler_params=pltpu.CompilerParams(vmem_limit_bytes=12 << 20),
        name="strips",
    )(state, adj, land_mask, from_south, from_north)
    from_west = lax.ppermute(to_east, "lon", [(i, (i + 1) % 16) for i in range(16)])
    from_east = lax.ppermute(to_west, "lon", [((i + 1) % 16, i) for i in range(16)])

    pairs = (2, LANES)
    payload = pl.pallas_call(
        payload_kernel,
        out_shape=pltpu.HBM((TILES, 40, LANES), f32),
        in_specs=[vmem()] * 7 + [pl.BlockSpec(memory_space=pl.ANY)] * 2,
        out_specs=vmem(),
        compiler_params=pltpu.CompilerParams(vmem_limit_bytes=4 << 20),
        name="payload",
    )(flux, *sent, routes.reshape(pairs), dest_row.reshape(pairs), weight_id.reshape(pairs), from_south, from_north)
    gathered = lax.all_to_all(payload, ("lat", "lon"), split_axis=0, concat_axis=0, tiled=True)
    gathered = gathered.reshape(TILES * 40, LANES)

    wide = (ADJ_ROWS, WIDE)
    matrix = (12 * ADJ_ROWS, 1024)
    result = pl.pallas_call(
        ocean_kernel,
        out_shape=shape_of((FLD, LEVB, ROWS, COLS)),
        in_specs=[in_hbm()] * 8 + [vmem()] * 5,
        out_specs=pl.BlockSpec(memory_space=pl.ANY),
        scratch_shapes=[
            SM((FLD,), f32),
            SM((FLD,), f32),
            SM((4, 8), f32),
            VM((512, 512), bf16),
            VM((512, 256), bf16),
            VM((ROWS, COLS), jnp.int32),
            VM((2, PLANES, HALO_ROWS, WIDE), f32),
            VM((FLD, LEVB) + wide, f32),
            VM((HALO_ROWS, WIDE), f32),
            VM(wide, f32),
            VM((NSTEP, LEVB) + wide, f32),
            VM((NSTEP, LEVB) + wide, f32),
            VM((NSTEP, FLD, LEVB) + wide, f32),
            VM((NSTEP, FLD, LEVB) + wide, f32),
            VM(matrix, bf16),
            VM(matrix, bf16),
            VM((3, LANES, LANES), f32),
            VM((4, LANES, LANES), f32),
            VM((8, 12, ADJ_ROWS, LANES), f32),
            VM((1024, COLS), bf16),
            VM((1024, COLS), bf16),
            VM((FLD, LEVB, ROWS, COLS), f32),
            pltpu.SemaphoreType.DMA((6 + 2 * PLANES,)),
        ],
        compiler_params=pltpu.CompilerParams(vmem_limit_bytes=48 << 20),
        name="ocean",
    )(
        *[hbm(x) for x in (diffusivity, penetration, regrid_table.T, *spread_tables(), state, adj, land_mask)],
        from_south,
        from_north,
        from_west,
        from_east,
        gathered,
    )
    return result[None]


def solution(mesh):
    in_specs = (
        P("comp", None, None, "lat", "lon"),
        P("comp", None, None, "lat", "lon"),
        P("lat", "lon"),
        P(),
        P(),
        P(),
        P(("lat", "lon"), None),
        P(("lat", "lon")),
        P(("lat", "lon")),
        P(),
    )
    out_specs = P("comp", None, None, "lat", "lon")
    return jax.shard_map(shards, mesh=mesh, in_specs=in_specs, out_specs=out_specs, check_vma=False)
```

time: 120 us -> 71 us (0.59); the launches traced: 118 us -> 70.3 us
  local copies, waits for them, and re-layouts: 35 us -> 0.02 us
  starting transfers between devices: 29.6 us -> 20.6 us
  Pallas kernels: 26.1 us -> 24.3 us
    unnamed x67 -> x12, local copies, waits for them, and re-layouts: 32 us -> 0.02 us
    ppermute x1, waiting for transfers between devices: 11 us -> 0.01 us  [shards(): from_south = lax.ppermute(to_north, 'lat', [(i, i + 1) for i in range(3)])]
    all_to_all x2 -> x1, waiting for transfers between devices: 0.01 us -> 9.95 us  [shards(): lax.all_to_all(payload, ('lat', 'lon'), split_axis=0, concat_axis=0, tile...]
    all_to_all x2 -> x1, starting transfers between devices: 20.5 us -> 11 us  [shards(): lax.all_to_all(payload, ('lat', 'lon'), split_axis=0, concat_axis=0, tile...]
    ppermute x1, waiting for transfers between devices: 1.04 us -> 8.67 us  [shards(): lax.ppermute(to_east, 'lon', [(i, (i + 1) % 16) for i in range(16)])]
    broadcast_in_dim x5 -> x0, local copies, waits for them, and re-layouts: 2.9 us -> none  [the longest x1 1.1 us: shards(): jnp.broadcast_to(here[None], (TILES, 32, LANES))]
    ppermute x3, waiting for transfers between devices: 9.25 us -> 6.43 us  [shards(): sent = [lax.ppermute(flux, 'comp', [(3, band)]) for band in range(3)]]
    ppermute x1, waiting for transfers between devices: 2.57 us -> 0.01 us  [shards(): lax.ppermute(to_west, 'lon', [((i + 1) % 16, i) for i in range(16)])]
  transfers between devices with their start and end apart: 9 -> 8, of which waited for: 5 -> 3; matrix products, arithmetic and copies ran while one was open for 2% -> 0% of each run, Pallas kernels for 16% -> 1%
where the time goes in v1:
time: 71 us; the launch traced here: 70.3 us
  waiting for transfers between devices  25.1 us (35%)
  Pallas kernels  24.3 us (34%)
  starting transfers between devices  20.6 us (29%)
    pallas_call x1, Pallas kernels, shards(): pl.pallas_call(ocean_kernel, out_shape=shape_of((FLD, LEVB, ROWS, COLS)),...  20.1 us
    all_to_all x1, starting transfers between devices, shards(): lax.all_to_all(payload, ('lat', 'lon'), split_axis=0, concat_axis=0, tile...  11 us
    all_to_all x1, waiting for transfers between devices, shards(): lax.all_to_all(payload, ('lat', 'lon'), split_axis=0, concat_axis=0, tile...  9.95 us
    ppermute x1, waiting for transfers between devices, shards(): lax.ppermute(to_east, 'lon', [(i, (i + 1) % 16) for i in range(16)])  8.67 us
    ppermute x3, waiting for transfers between devices, shards(): sent = [lax.ppermute(flux, 'comp', [(3, band)]) for band in range(3)]  6.43 us
    ppermute x1, starting transfers between devices, shards(): from_south = lax.ppermute(to_north, 'lat', [(i, i + 1) for i in range(3)])  3.96 us
    ppermute x3, starting transfers between devices, shards(): sent = [lax.ppermute(flux, 'comp', [(3, band)]) for band in range(3)]  2.62 us
    pallas_call x1, Pallas kernels, shards(): pl.pallas_call(flux_kernel, out_shape=(shape_of((32, LANES)), edge, edge)...  2.21 us
  transfers between devices with their start and end apart: 8, of which 3 were waited for; matrix products, arithmetic and copies ran while one was open for 0% of the time, Pallas kernels for 1%

profile of v1, /device:TPU:1, one launch (start us, length us, event | category | flops | bytes accessed | tf_op | source)
XLA Modules:
  0.0 70.3 jit_solution(4757991015004707169)
XLA Ops:
  0.0 0.0 copy-start.3
  0.0 0.0 copy-start.4
  0.0 0.0 copy-start.5
  0.0 2.2 %flux.1 = (f32[32,128]{1,0:T(8,128)S(1)}, f32[25,8,256]{2,1,0:T(8,128)}, f32[25,8,256]{2,1,0:T(8,128)}) custom-call(f32[6,2,64,256]{3,2,1,0:T(8,128)} %bitcast.8, f32[6,2,64,256]{3,2,1,0:T(8,128)} %bitcast.11, s32[64,256]{1,0:T(8,128)} %mask.5, f32[4,192]{1,0:T(4,128)} %weight.1), custom_call_target="tpu_custom_call" | custom-call | tf_op jit(solution)/shard_map/flux/pallas_call | solution.py:455
  2.2 4.0 %collective-permute-start = (f32[25,8,256]{2,1,0:T(8,128)}, f32[25,8,256]{2,1,0:T(8,128)S(1)}, u32[]{:S(2)}, u32[]{:S(2)}) collective-permute-start(f32[25,8,256]{2,1,0:T(8,128)} %get-tuple-element.10), channel_id=1, source_target_pairs={{0,16},{16,32},{32,48},{1,17},{17,33},{33,49},{2,18},{18,34},{34,5... | collective-permute-start | bytes 614408 | tf_op jit(solution)/shard_map/ppermute | solution.py:471
  6.2 1.3 %collective-permute-start.1 = (f32[25,8,256]{2,1,0:T(8,128)}, f32[25,8,256]{2,1,0:T(8,128)S(1)}, u32[]{:S(2)}, u32[]{:S(2)}) collective-permute-start(f32[25,8,256]{2,1,0:T(8,128)} %get-tuple-element.11), channel_id=1, source_target_pairs={{16,0},{32,16},{48,32},{17,1},{33,17},{49,33},{18,2},{34,18},{50,3... | collective-permute-start | bytes 614408 | tf_op jit(solution)/shard_map/ppermute | solution.py:472
  7.5 1.3 %collective-permute-start.4 = (f32[32,128]{1,0:T(8,128)S(1)}, f32[32,128]{1,0:T(8,128)S(1)}, u32[]{:S(2)}, u32[]{:S(2)}) collective-permute-start(f32[32,128]{1,0:T(8,128)S(1)} %get-tuple-element.14.flux), channel_id=1, source_target_pairs={{192,0},{193,1},{194,2},{195,3},{196,4},{197,5},{198,6},{199,7},{2... | collective-permute-start | bytes 49160 | tf_op jit(solution)/shard_map/ppermute | solution.py:470
  8.8 0.7 collective-permute-start.5
  9.5 0.7 collective-permute-start.6
  10.1 6.4 %collective-permute-done.4.first = f32[32,128]{1,0:T(8,128)S(1)} collective-permute-done((f32[32,128]{1,0:T(8,128)S(1)}, f32[32,128]{1,0:T(8,128)S(1)}, u32[]{:S(2)}, u32[]{:S(2)}) %collective-permute-start.4) | collective-permute-done | bytes 16416 | tf_op jit(solution)/shard_map/ppermute | solution.py:470
  16.6 0.0 collective-permute-done.5.second
  16.6 0.0 collective-permute-done.6.third
  16.6 0.0 collective-permute-done.from_south
  16.6 0.0 collective-permute-done.1.from_north
  16.6 0.0 copy-done.3
  16.6 0.0 copy-done.4
  16.6 0.0 copy-done.5
  16.6 1.4 %payload.1 = f32[64,40,128]{2,1,0:T(8,128)} custom-call(f32[32,128]{1,0:T(8,128)S(1)} %get-tuple-element.14.flux, f32[32,128]{1,0:T(8,128)S(1)} %collective-permute-done.4.first, f32[32,128]{1,0:T(8,128)S(1)} %collective-permute-done.5.second, f32[32,128]{1,0:T(8,128)S(1)} %collective-permute-done.6.third, s32[2,128]{1,0:T(2,128)S(1)} %bitcast.15, ...), custom_call_target="tpu_custom_call" | custom-call | tf_op jit(solution)/shard_map/payload/pallas_call | solution.py:487
  18.1 0.0 copy-start
  18.1 0.0 copy-start.1
  18.1 0.0 copy-start.2
  18.1 11.0 %all-to-all-start = ((f32[64,40,128]{2,1,0:T(8,128)}), f32[64,40,128]{2,1,0:T(8,128)S(1)}, u32[]{:S(2)}, u32[]{:S(2)}) async-start(f32[64,40,128]{2,1,0:T(8,128)} %payload.1), calls=%async_computation | async-start | bytes 2621440 | tf_op jit(solution)/shard_map/all_to_all | solution.py:495
  29.1 0.0 copy-done
  29.1 0.0 copy-done.1
  29.1 0.0 copy-done.2
  29.1 0.6 strips.1
  29.7 1.7 %collective-permute-start.2 = (f32[2,80,128]{2,1,0:T(8,128)S(1)}, f32[2,80,128]{2,1,0:T(8,128)S(1)}, u32[]{:S(2)}, u32[]{:S(2)}) collective-permute-start(f32[2,80,128]{2,1,0:T(8,128)S(1)} %get-tuple-element.12), channel_id=1, source_target_pairs={{0,1},{1,2},{2,3},{3,4},{4,5},{5,6},{6,7},{7,8},{8,9},{9,10},{10,1... | collective-permute-start | bytes 245768 | tf_op jit(solution)/shard_map/ppermute | solution.py:483
  31.4 0.0 collective-permute-start.3
  31.4 8.7 %collective-permute-done.2.from_west = f32[2,80,128]{2,1,0:T(8,128)S(1)} collective-permute-done((f32[2,80,128]{2,1,0:T(8,128)S(1)}, f32[2,80,128]{2,1,0:T(8,128)S(1)}, u32[]{:S(2)}, u32[]{:S(2)}) %collective-permute-start.2) | collective-permute-done | bytes 81952 | tf_op jit(solution)/shard_map/ppermute | solution.py:483
  40.1 0.0 collective-permute-done.3.from_east
  40.1 9.9 %all-to-all-done = f32[64,40,128]{2,1,0:T(8,128)S(1)} async-done(((f32[64,40,128]{2,1,0:T(8,128)}), f32[64,40,128]{2,1,0:T(8,128)S(1)}, u32[]{:S(2)}, u32[]{:S(2)}) %all-to-all-start) | async-done | bytes 1310752 | tf_op jit(solution)/shard_map/all_to_all | solution.py:495
  50.1 20.1 %ocean.1 = f32[6,2,64,256]{3,2,1,0:T(8,128)} custom-call(f32[6]{0:T(128)} %diffusivity_at.1, f32[6]{0:T(128)} %penetration_at.1, f32[4,8]{1,0:T(4,128)} %bitcast.18, bf16[512,512]{1,0:T(8,128)(2,1)} %constant.4.clone.spread_own_at, bf16[512,256]{1,0:T(8,128)(2,1)} %constant.5.clone.spread_side_at, f32[6,2,64,256]{3,2,1,0:T(8,128)} %bitcast.9, ...), custom_call_target="tpu_custom_call" | custom-call | tf_op jit(solution)/shard_map/ocean/pallas_call | solution.py:500
Async XLA Ops:
  0.0 16.6 %copy-start.3 = (s32[256,1]{0,1:T(1,128)S(1)}, s32[256,1]{0,1:T(1,128)}, u32[]{:S(2)}) copy-start(s32[256,1]{0,1:T(1,128)} %param.18) | copy-start | bytes 3076
  0.0 16.6 %copy-start.4 = (s32[256]{0:T(256)S(1)}, s32[256]{0:T(256)}, u32[]{:S(2)}) copy-start(s32[256]{0:T(256)} %param.19) | copy-start | bytes 3076
  0.0 16.6 %copy-start.5 = (s32[256]{0:T(256)S(1)}, s32[256]{0:T(256)}, u32[]{:S(2)}) copy-start(s32[256]{0:T(256)} %param.20) | copy-start | bytes 3076
  2.2 14.3 %collective-permute-start = (f32[25,8,256]{2,1,0:T(8,128)}, f32[25,8,256]{2,1,0:T(8,128)S(1)}, u32[]{:S(2)}, u32[]{:S(2)}) collective-permute-start(f32[25,8,256]{2,1,0:T(8,128)} %get-tuple-element.10), channel_id=1, source_target_pairs={{0,16},{16,32},{32,48},{1,17},{17,33},{33,49},{2,18},{18,34},{34,5... | collective-permute-start | bytes 614408 | tf_op jit(solution)/shard_map/ppermute | solution.py:471
  6.2 10.4 %collective-permute-start.1 = (f32[25,8,256]{2,1,0:T(8,128)}, f32[25,8,256]{2,1,0:T(8,128)S(1)}, u32[]{:S(2)}, u32[]{:S(2)}) collective-permute-start(f32[25,8,256]{2,1,0:T(8,128)} %get-tuple-element.11), channel_id=1, source_target_pairs={{16,0},{32,16},{48,32},{17,1},{33,17},{49,33},{18,2},{34,18},{50,3... | collective-permute-start | bytes 614408 | tf_op jit(solution)/shard_map/ppermute | solution.py:472
  7.5 9.1 %collective-permute-start.4 = (f32[32,128]{1,0:T(8,128)S(1)}, f32[32,128]{1,0:T(8,128)S(1)}, u32[]{:S(2)}, u32[]{:S(2)}) collective-permute-start(f32[32,128]{1,0:T(8,128)S(1)} %get-tuple-element.14.flux), channel_id=1, source_target_pairs={{192,0},{193,1},{194,2},{195,3},{196,4},{197,5},{198,6},{199,7},{2... | collective-permute-start | bytes 49160 | tf_op jit(solution)/shard_map/ppermute | solution.py:470
  8.8 7.8 %collective-permute-start.5 = (f32[32,128]{1,0:T(8,128)S(1)}, f32[32,128]{1,0:T(8,128)S(1)}, u32[]{:S(2)}, u32[]{:S(2)}) collective-permute-start(f32[32,128]{1,0:T(8,128)S(1)} %get-tuple-element.14.flux), channel_id=1, source_target_pairs={{192,64},{193,65},{194,66},{195,67},{196,68},{197,69},{198,70},{19... | collective-permute-start | bytes 49160 | tf_op jit(solution)/shard_map/ppermute | solution.py:470
  9.5 7.1 %collective-permute-start.6 = (f32[32,128]{1,0:T(8,128)S(1)}, f32[32,128]{1,0:T(8,128)S(1)}, u32[]{:S(2)}, u32[]{:S(2)}) collective-permute-start(f32[32,128]{1,0:T(8,128)S(1)} %get-tuple-element.14.flux), channel_id=1, source_target_pairs={{192,128},{193,129},{194,130},{195,131},{196,132},{197,133},{198,1... | collective-permute-start | bytes 49160 | tf_op jit(solution)/shard_map/ppermute | solution.py:470
  18.1 11.1 %copy-start = (f32[1,6,2,64,256]{4,3,2,1,0:T(8,128)S(1)}, f32[1,6,2,64,256]{4,3,2,1,0:T(8,128)}, u32[]{:S(2)}) copy-start(f32[1,6,2,64,256]{4,3,2,1,0:T(8,128)} %param.12) | copy-start | bytes 2359300
  18.1 11.1 %copy-start.1 = (f32[1,6,2,64,256]{4,3,2,1,0:T(8,128)S(1)}, f32[1,6,2,64,256]{4,3,2,1,0:T(8,128)}, u32[]{:S(2)}) copy-start(f32[1,6,2,64,256]{4,3,2,1,0:T(8,128)} %param.13) | copy-start | bytes 2359300
  18.1 11.1 %copy-start.2 = (s32[64,256]{1,0:T(8,128)S(1)}, s32[64,256]{1,0:T(8,128)}, u32[]{:S(2)}) copy-start(s32[64,256]{1,0:T(8,128)} %mask.5) | copy-start | bytes 196612
  18.1 32.0 %all-to-all-start = ((f32[64,40,128]{2,1,0:T(8,128)}), f32[64,40,128]{2,1,0:T(8,128)S(1)}, u32[]{:S(2)}, u32[]{:S(2)}) async-start(f32[64,40,128]{2,1,0:T(8,128)} %payload.1), calls=%async_computation | async-start | bytes 2621440 | tf_op jit(solution)/shard_map/all_to_all | solution.py:495
  29.7 10.4 %collective-permute-start.2 = (f32[2,80,128]{2,1,0:T(8,128)S(1)}, f32[2,80,128]{2,1,0:T(8,128)S(1)}, u32[]{:S(2)}, u32[]{:S(2)}) collective-permute-start(f32[2,80,128]{2,1,0:T(8,128)S(1)} %get-tuple-element.12), channel_id=1, source_target_pairs={{0,1},{1,2},{2,3},{3,4},{4,5},{5,6},{6,7},{7,8},{8,9},{9,10},{10,1... | collective-permute-start | bytes 245768 | tf_op jit(solution)/shard_map/ppermute | solution.py:483
  31.4 8.7 %collective-permute-start.3 = (f32[2,80,128]{2,1,0:T(8,128)S(1)}, f32[2,80,128]{2,1,0:T(8,128)S(1)}, u32[]{:S(2)}, u32[]{:S(2)}) collective-permute-start(f32[2,80,128]{2,1,0:T(8,128)S(1)} %get-tuple-element.13), channel_id=1, source_target_pairs={{1,0},{2,1},{3,2},{4,3},{5,4},{6,5},{7,6},{8,7},{9,8},{10,9},{11,1... | collective-permute-start | bytes 245768 | tf_op jit(solution)/shard_map/ppermute | solution.py:484

commit v2 on v1

v2 whole, which is shorter than its diff:
```python
import jax
import jax.numpy as jnp
import ml_dtypes
import numpy as np
from jax import lax
from jax.experimental import pallas as pl
from jax.experimental.pallas import tpu as pltpu
from jax.sharding import PartitionSpec as P

NSTEP = 4
STEP_COEF = 0.2
SPEED_BASE = 0.5
SPEED_GAIN = 0.5

FLD = 6
NFLUX = 4
LEVB = 2
ROWS = 64
COLS = 256
PLANES = FLD * LEVB
HALO_ROWS = 80
ADJ_ROWS = 72
WIDE = 384
LANES = 128
TILES = 64
SEGS = 16
FAR = -1.0

f32 = jnp.float32
bf16 = jnp.bfloat16
VM = pltpu.VMEM
SM = pltpu.SMEM


def vmem():
    return pl.BlockSpec(memory_space=VM)


def smem():
    return pl.BlockSpec(memory_space=SM)


def in_hbm():
    return pl.BlockSpec(memory_space=pltpu.HBM)


def hbm(x):
    return pltpu.with_memory_space_constraint(jnp.asarray(x), pltpu.HBM)


def shape_of(shape, dtype=f32):
    return jax.ShapeDtypeStruct(shape, dtype)


def east(x):
    return pltpu.roll(x, WIDE - 1, 1)


def west(x):
    return pltpu.roll(x, 1, 1)


def north(x):
    return pltpu.roll(x, x.shape[0] - 1, 0)


def south(x):
    return pltpu.roll(x, 1, 0)


def iota(shape, dim):
    return lax.broadcasted_iota(jnp.int32, shape, dim)


def split(x):
    high = x.astype(bf16)
    return high, (x - high.astype(f32)).astype(bf16)


def dot(x, y):
    return jnp.dot(x, y, preferred_element_type=f32)


def exact_parts(x):
    head = x.astype(bf16).astype(f32)
    rest = x - head
    middle = rest.astype(bf16).astype(f32)
    return [head, middle, rest - middle]


def packed_strips(planes_west, planes_east):
    lane_group = iota(planes_west[0].shape, 1) // 8
    east_strip = jnp.zeros(planes_west[0].shape, f32)
    west_strip = east_strip
    for plane, (edge_w, edge_e) in enumerate(zip(planes_west, planes_east)):
        east_strip = jnp.where(lane_group == plane, pltpu.roll(edge_e, 8 * plane + 8, 1), east_strip)
        moved = pltpu.roll(edge_w, 8 * plane, 1) if plane else edge_w
        west_strip = jnp.where(lane_group == plane, moved, west_strip)
    return east_strip, west_strip


def flux_kernel(
    checkpoint,
    adjoint_in,
    mask,
    weight,
    flux,
    to_north,
    to_south,
    own_east,
    own_west,
    held,
    held_adj,
    held_mask,
    held_weight,
    sems,
):
    pairs = ((checkpoint, held), (adjoint_in, held_adj), (mask, held_mask), (weight, held_weight))
    copies = [pltpu.make_async_copy(source, target, sems.at[at]) for at, (source, target) in enumerate(pairs)]
    for copy in copies:
        copy.start()

    @pl.when(lax.axis_index("comp") != 3)
    def _():
        flux[...] = jnp.zeros((40, LANES), f32)
        for copy in copies:
            copy.wait()
        top, low = slice(ROWS - 8, ROWS), slice(0, 8)
        row = iota((8, COLS), 0)
        for f in range(FLD):
            for l in range(LEVB):
                to_north[f * LEVB + l] = held[f, l, top, :]
                to_south[f * LEVB + l] = held[f, l, low, :]
            upper = pltpu.roll(held_adj[f, 1, top, :], 4, 0)
            to_north[PLANES + f] = jnp.where(row < 4, upper, held_adj[f, 0, top, :])
            lower = pltpu.roll(held_adj[f, 1, low, :], 4, 0)
            to_south[PLANES + f] = jnp.where(row < 4, held_adj[f, 0, low, :], lower)
        to_north[PLANES + FLD] = held_mask[top, :].astype(f32)
        to_south[PLANES + FLD] = held_mask[low, :].astype(f32)
        for kind, source in enumerate((held, held_adj)):
            planes = [source[plane // LEVB, plane % LEVB] for plane in range(PLANES)]
            if kind == 0:
                planes.append(held_mask[...].astype(f32))
            own_east[kind], own_west[kind] = packed_strips([x[:, 0:LANES] for x in planes], [x[:, LANES:] for x in planes])

    @pl.when(lax.axis_index("comp") == 3)
    def _():
        copies[3].wait()
        w = held_weight[...]
        parts = jnp.concatenate(exact_parts(w) + [jnp.zeros_like(w)], axis=0).astype(bf16)
        level, row = iota((FLD * 32, PLANES * ROWS), 0), iota((FLD * 32, PLANES * ROWS), 1)
        repeated = dot(parts, jnp.where(row // 4 == level, 1.0, 0.0).astype(bf16))
        repeated = repeated[0:4] + repeated[4:8] + repeated[8:12]
        own = iota((4, PLANES * ROWS), 1) % 4 == iota((4, PLANES * ROWS), 0)
        spread = jnp.concatenate([jnp.where(own, repeated[k : k + 1], 0.0) for k in range(NFLUX)], axis=0)
        for copy in copies[:3]:
            copy.wait()
        t = jnp.tanh(held[...])
        sens = (held_adj[...] * (1.0 - t * t)).reshape(PLANES * ROWS, COLS)
        by_kind = jnp.dot(spread, sens, precision=lax.Precision.HIGHEST, preferred_element_type=f32)
        rows = []
        for q in range(4):
            rows.append(
                jnp.concatenate(
                    [by_kind[k * 4 : k * 4 + 4, q * 64 : q * 64 + 64] for k in range(NFLUX)], axis=1
                )
            )
        by_seg = jnp.concatenate(rows, axis=0)
        flux[0:16, :] = by_seg[:, 0:LANES]
        flux[16:32, :] = by_seg[:, LANES:]
        lane = iota((COLS, LANES), 1)
        pick = jnp.where(iota((COLS, LANES), 0) == (lane % 4) * 64 + 63 * (lane // 64), 1.0, 0.0).astype(bf16)
        ends = dot(jnp.concatenate(exact_parts(by_kind), axis=0).astype(bf16), pick)
        ends = ends[0:16] + ends[16:32] + ends[32:48]
        lane = iota((16, LANES), 1)
        mine = iota((16, LANES), 0) == (lane // 16 % 4) * 4 + lane // 4 % 4
        flux[32:33, :] = jnp.sum(jnp.where(mine, ends, 0.0), axis=0, keepdims=True)
        flux[33:40, :] = jnp.zeros((7, LANES), f32)


def adjoint_halo(from_north, from_south, f, l):
    high, low = from_north[PLANES + f], from_south[PLANES + f]
    if l:
        high, low = pltpu.roll(high, 4, 0), pltpu.roll(low, 4, 0)
    return jnp.where(iota((8, COLS), 0) < 4, high, low)


def strip_kernel(own_east, own_west, from_south, from_north, to_east, to_west):
    states = [jnp.concatenate([from_north[p], from_south[p]], axis=0) for p in range(PLANES)]
    states.append(jnp.concatenate([from_north[PLANES + FLD], from_south[PLANES + FLD]], axis=0))
    adjoints = [adjoint_halo(from_north, from_south, p // LEVB, p % LEVB) for p in range(PLANES)]
    for target, own in ((to_east, own_east), (to_west, own_west)):
        target[0:ROWS, :] = own[0]
        target[HALO_ROWS : HALO_ROWS + ROWS, :] = own[1]
    for start, planes in ((ROWS, states), (HALO_ROWS + ROWS, adjoints)):
        rows = slice(start, start + planes[0].shape[0])
        to_east[rows, :], to_west[rows, :] = packed_strips([x[:, 0:LANES] for x in planes], [x[:, LANES:] for x in planes])


def payload_kernel(flux, first, second, third, routes, dest_row, weight_id, south, north, payload, block, lists, sems):
    del south, north
    copies = [
        pltpu.make_async_copy(x, lists.at[pl.ds(2 * at, 2)], sems.at[at])
        for at, x in enumerate((routes, dest_row, weight_id))
    ]
    for copy in copies:
        copy.start()
    block[...] = flux[...] + (first[...] + second[...] + third[...])
    for copy in copies:
        copy.wait()
    block[33:39, :] = lists[0:6, :].astype(f32)
    copies = [pltpu.make_async_copy(block, payload.at[tile], sems.at[tile]) for tile in range(TILES)]
    for copy in copies:
        copy.start()
    for copy in copies:
        copy.wait()


def to_adjoint_rows(x):
    row = iota((8, WIDE), 0)
    return jnp.concatenate([x[0:ROWS], jnp.where(row < 4, x[ROWS : ROWS + 8], x[ROWS + 8 :])], axis=0)


def pulled(mu, a, b, d):
    mixed, carried_e, carried_n = d * mu, a * mu, b * mu
    return (
        (1.0 - 4.0 * d) * mu
        + (east(mixed + carried_e) + west(mixed - carried_e))
        + (north(mixed + carried_n) + south(mixed - carried_n))
    )


def route_matrix(gathered, table, widen, high, low, code_t, prof_t, total, products, side_code):
    lat_me, lon_me = lax.axis_index("lat"), lax.axis_index("lon")

    def listed(at):
        parts = [gathered[pl.ds(33 + 2 * at + half, TILES, stride=40), :] for half in range(2)]
        return jnp.concatenate(parts, axis=1).astype(jnp.int32)

    def stacked(x):
        return jnp.concatenate([x[:, 0:LANES], x[:, LANES:]], axis=0)

    dest, row, profile = listed(0), listed(1), listed(2)
    dest_lat, dest_lon = jnp.right_shift(dest, 4), jnp.bitwise_and(dest, 15)
    row = row + ROWS * (dest_lat - lat_me)
    valid = jnp.logical_and(row >= -4, row < ROWS + 4)
    code = jnp.where(row < 0, row + ADJ_ROWS, row)
    is_east = dest_lon == (lon_me + 1) % 16
    is_west = dest_lon == (lon_me + 15) % 16
    own_code = jnp.where(jnp.logical_and(valid, dest_lon == lon_me), code.astype(f32), FAR)
    code_t[...] = stacked(own_code).T
    off = jnp.where(is_east, code, jnp.where(is_west, code + ADJ_ROWS, -1))
    side_code[...] = jnp.where(valid, off, -1).astype(f32)
    ends = jnp.concatenate(exact_parts(gathered[pl.ds(32, TILES, stride=40), :]), axis=0).astype(bf16)
    ends = dot(ends, widen[...])
    ends = ends[0:TILES] + ends[TILES : 2 * TILES] + ends[2 * TILES :]
    for c in range(4):
        weights = jnp.zeros((TILES, COLS), f32)
        for w in range(8):
            weights = jnp.where(profile == w, table[c, w], weights)
        prof_t[c] = stacked(weights).T
        for k in range(NFLUX):
            first, final = ends[:, k * COLS : (k + 1) * COLS], ends[:, (4 + k) * COLS : (5 + k) * COLS]
            at = (k * 4 + c) * TILES
            product = weights * jnp.where(is_east, first, final)
            products[0, at : at + TILES, :] = product[:, 0:LANES]
            products[1, at : at + TILES, :] = product[:, LANES:]
    own_matrix(code_t, prof_t, total, high, low)
    return side_sums(products, side_code)


def own_matrix(code_t, prof_t, total, high, low):
    rows = iota((ADJ_ROWS, LANES), 0).astype(f32)

    def build(seg, carry):
        sums = [jnp.zeros((ADJ_ROWS, LANES), f32) for _ in range(4)]
        for r in range(16):
            at = seg * 16 + r
            hit = code_t[pl.ds(at, 1), :] == rows
            for c in range(4):
                sums[c] = sums[c] + jnp.where(hit, prof_t[c, pl.ds(at, 1), :], 0.0)
        for c in range(4):
            total[seg, c] = sums[c]
        return carry

    lax.fori_loop(0, 8, build, 0)
    for seg in range(8):
        whole = total[seg].reshape(4 * ADJ_ROWS, LANES)
        head, tail = split(whole)
        high[:, seg * LANES : (seg + 1) * LANES] = head
        low[:, seg * LANES : (seg + 1) * LANES] = tail


def side_sums(products, side_code):
    bins = iota((2 * ADJ_ROWS, COLS), 0).astype(f32)

    def side(i, sums):
        for j in range(4):
            tile = i * 4 + j
            hit = jnp.where(side_code[pl.ds(tile, 1), :] == bins, 1.0, 0.0).astype(bf16)
            rows = pl.ds(tile, 16, stride=TILES)
            head, tail = split(jnp.concatenate([products[0, rows, :], products[1, rows, :]], axis=1))
            both = jnp.concatenate([head, tail], axis=0)
            sums = sums + lax.dot_general(hit, both, (((1,), (1,)), ((), ())), preferred_element_type=f32)
        return sums

    sums = lax.fori_loop(0, TILES // 4, side, jnp.zeros((2 * ADJ_ROWS, 32), f32))
    return sums[:, 0:16] + sums[:, 16:32]


def spread_tables():
    src, out = np.arange(512)[:, None], np.arange(512)[None, :]
    own = ((src // 64) % 2 == out // COLS) & (out % COLS == 4 * (src % 64) + src // 128)
    src, out = np.arange(LANES)[:, None], np.arange(8 * COLS)[None, :]
    seg = out % COLS // 16
    widen = (src // 16 == out // COLS) & (src % 16 == (seg // 4) * 4 + seg % 4)
    return own.astype(ml_dtypes.bfloat16), widen.astype(ml_dtypes.bfloat16)


def assemble_forcing(gathered, high, low, g_high, g_low, spread_own):
    for seg in range(8):
        for h in range(2):
            s = h * 8 + seg
            at = (s % 4) * 4 + s // 4
            for half in range(2):
                part = gathered[pl.ds(half * 16 + at, TILES, stride=40), :]
                head, tail = split(part)
                rows = slice(seg * LANES + h * 64, seg * LANES + h * 64 + 64)
                g_high[rows, half * LANES : (half + 1) * LANES] = head
                g_low[rows, half * LANES : (half + 1) * LANES] = tail
    coarse = dot(high[...], g_high[...]) + dot(high[...], g_low[...]) + dot(low[...], g_high[...])
    parts = []
    for half in range(2):
        cols = slice(half * LANES, (half + 1) * LANES)
        own = jnp.concatenate([coarse[c * ADJ_ROWS : (c + 1) * ADJ_ROWS, cols] for c in range(4)], axis=1)
        head = own.astype(bf16).astype(f32)
        parts += [head, own - head]
    return dot(jnp.concatenate(parts, axis=0).astype(bf16), spread_own[...])


def forward_steps(state, wet_all, diffusivity, speed_e, speed_n, grad_e, grad_n):
    for step in range(NSTEP):
        now, later = step % 2, (step + 1) % 2
        for l in range(LEVB):
            a = 0.5 * STEP_COEF * (SPEED_BASE + SPEED_GAIN * state[now, l])
            b = (0.5 * STEP_COEF * SPEED_GAIN) * state[now, LEVB + l]
            speed_e[step, l] = to_adjoint_rows(a)
            speed_n[step, l] = to_adjoint_rows(b)
            for f in range(FLD):
                d = diffusivity[f]
                q = state[now, f * LEVB + l]
                q_e, q_w, q_n, q_s = east(q), west(q), north(q), south(q)
                across, along = q_e - q_w, q_n - q_s
                half = -0.5 * STEP_COEF * SPEED_GAIN
                grad_e[step, f, l] = to_adjoint_rows(half * across)
                grad_n[step, f, l] = to_adjoint_rows(half * along)
                if step + 1 < NSTEP:
                    moved = (1.0 - 4.0 * d) * q + d * ((q_e + q_w) + (q_n + q_s)) - a * across - b * along
                    state[later, f * LEVB + l] = wet_all[...] * moved


def ocean_kernel(
    diffusivity_at,
    penetration_at,
    table_at,
    widen_at,
    spread_own_at,
    mask,
    checkpoint,
    adjoint_in,
    from_south,
    from_north,
    from_west,
    from_east,
    gathered,
    out,
    diffusivity,
    penetration,
    table,
    widen,
    spread_own,
    mask_own,
    state,
    lam,
    wet_all,
    wet,
    speed_e,
    speed_n,
    grad_e,
    grad_n,
    high,
    low,
    code_t,
    prof_t,
    total,
    products,
    side_code,
    g_high,
    g_low,
    done,
    sems,
):
    section = lax.axis_index("comp")
    pairs = [
        (diffusivity_at, diffusivity),
        (penetration_at, penetration),
        (table_at, table),
        (widen_at, widen),
        (spread_own_at, spread_own),
        (mask, mask_own),
    ]
    for plane in range(PLANES):
        f, l = plane // LEVB, plane % LEVB
        pairs.append((checkpoint.at[f, l], state.at[0, plane, 0:ROWS, 0:COLS]))
        pairs.append((adjoint_in.at[f, l], lam.at[f, l, 0:ROWS, 0:COLS]))
    copies = [pltpu.make_async_copy(source, target, sems.at[at]) for at, (source, target) in enumerate(pairs)]
    for copy in copies:
        copy.start()

    @pl.when(section == 3)
    def _():
        for copy in copies:
            copy.wait()
        for plane in range(PLANES):
            f, l = plane // LEVB, plane % LEVB
            t = jnp.tanh(state[0, plane, 0:ROWS, 0:COLS])
            done[f, l] = lam[f, l, 0:ROWS, 0:COLS] * (1.0 - t * t)

    @pl.when(section != 3)
    def _():
        for copy in copies[:5]:
            copy.wait()
        sides = route_matrix(gathered, table, widen, high, low, code_t, prof_t, total, products, side_code)
        own = assemble_forcing(gathered, high, low, g_high, g_low, spread_own)

        def edge(start, rows, plane):
            lane = iota((rows, LANES), 1)
            west_side, east_side = from_west[start : start + rows], from_east[start : start + rows]
            if plane:
                east_side = pltpu.roll(east_side, LANES - 8 * plane, 1)
            west_side = pltpu.roll(west_side, (120 - 8 * plane) % LANES, 1)
            return jnp.where(lane < 8, east_side, jnp.where(lane >= 120, west_side, 0.0))

        for f in range(FLD):
            for l in range(LEVB):
                plane = f * LEVB + l
                state[0, plane, ROWS : ROWS + 8, 0:COLS] = from_north[plane]
                state[0, plane, ROWS + 8 :, 0:COLS] = from_south[plane]
                state[0, plane, :, COLS:] = edge(0, HALO_ROWS, plane)
                lam[f, l, ROWS:, 0:COLS] = adjoint_halo(from_north, from_south, f, l)
                lam[f, l, :, COLS:] = edge(HALO_ROWS, ADJ_ROWS, plane)
        at = PLANES + FLD
        for copy in copies[5:]:
            copy.wait()
        wet_all[0:ROWS, 0:COLS] = mask_own[...].astype(f32)
        wet_all[ROWS : ROWS + 8, 0:COLS] = from_north[at]
        wet_all[ROWS + 8 :, 0:COLS] = from_south[at]
        wet_all[:, COLS:] = edge(0, HALO_ROWS, PLANES)
        wet[...] = to_adjoint_rows(wet_all[...])
        lane = iota((ADJ_ROWS, LANES), 1)
        sides = jnp.concatenate([sides, jnp.zeros((2 * ADJ_ROWS, LANES - 16), f32)], axis=1)
        w = wet[...]
        band = lax.axis_index("comp")
        for k in range(NFLUX):
            at, sub = (k // 2) * 2 * ADJ_ROWS, k % 2
            own_k = own[:, sub * COLS : (sub + 1) * COLS]
            own_k = own_k[at : at + ADJ_ROWS] + own_k[at + ADJ_ROWS : at + 2 * ADJ_ROWS]
            first, final = sides[0:ADJ_ROWS], sides[ADJ_ROWS:]
            if k:
                first = pltpu.roll(first, LANES - 4 * k, 1)
            final = pltpu.roll(final, LANES - 4 * k - 4, 1)
            side_k = jnp.where(lane < 4, first, jnp.where(lane >= LANES - 4, final, 0.0))
            forcing = w * jnp.concatenate([own_k, side_k], axis=1)
            for l in range(LEVB):
                lam[k, l] = lam[k, l] + penetration[band * LEVB + l] * forcing

        forward_steps(state, wet_all, diffusivity, speed_e, speed_n, grad_e, grad_n)

        def back(i, carry):
            step = NSTEP - 1 - i
            for l in range(LEVB):
                a, b, w = speed_e[step, l], speed_n[step, l], wet[...]
                sum_e, sum_n = 0.0, 0.0
                for f in (2, 3, 4, 5, 1, 0):
                    mu = w * lam[f, l]
                    sum_e = sum_e + mu * grad_e[step, f, l]
                    sum_n = sum_n + mu * grad_n[step, f, l]
                    lam[f, l] = pulled(mu, a, b, diffusivity[f])
                lam[0, l] = lam[0, l] + sum_e
                lam[1, l] = lam[1, l] + sum_n
            return carry

        lax.fori_loop(0, NSTEP, back, 0)
        for f in range(FLD):
            for l in range(LEVB):
                done[f, l] = lam[f, l, 0:ROWS, 0:COLS]

    copy = pltpu.make_async_copy(done, out, sems.at[0])
    copy.start()
    copy.wait()


def shards(
    checkpoint,
    adjoint_in,
    land_mask,
    diffusivity,
    penetration,
    column_weight,
    routes,
    dest_row,
    weight_id,
    regrid_table,
):
    state, adj = checkpoint[0], adjoint_in[0]
    state_at, adj_at, mask_at = hbm(state), hbm(adj), hbm(land_mask)
    any_place = pl.BlockSpec(memory_space=pl.ANY)
    held = VM((FLD, LEVB, ROWS, COLS), f32)
    edge = shape_of((PLANES + FLD + 1, 8, COLS))
    own_strip = shape_of((2, ROWS, LANES))
    pairs = (2, LANES)
    small = pltpu.CompilerParams(vmem_limit_bytes=2 << 20)
    flux, to_north, to_south, own_east, own_west = pl.pallas_call(
        flux_kernel,
        out_shape=(shape_of((40, LANES)), edge, edge, own_strip, own_strip),
        in_specs=[in_hbm()] * 4,
        out_specs=(vmem(),) * 5,
        scratch_shapes=[
            held,
            held,
            VM((ROWS, COLS), jnp.int32),
            VM((NFLUX, FLD * 32), f32),
            pltpu.SemaphoreType.DMA((4,)),
        ],
        compiler_params=pltpu.CompilerParams(vmem_limit_bytes=12 << 20),
        name="flux",
    )(
        state_at,
        adj_at,
        mask_at,
        hbm(column_weight),
    )
    sent = [lax.ppermute(flux, "comp", [(3, band)]) for band in range(3)]
    rows_up = [(c * 4 + i, c * 4 + i + 1) for c in range(3) for i in range(3)]
    from_south = lax.ppermute(to_north, ("comp", "lat"), rows_up)
    from_north = lax.ppermute(to_south, ("comp", "lat"), [(b, a) for a, b in rows_up])

    payload = pl.pallas_call(
        payload_kernel,
        out_shape=pltpu.HBM((TILES, 40, LANES), f32),
        in_specs=[vmem()] * 4 + [in_hbm()] * 3 + [any_place] * 2,
        out_specs=in_hbm(),
        scratch_shapes=[VM((40, LANES), f32), VM((8, LANES), jnp.int32), pltpu.SemaphoreType.DMA((TILES,))],
        compiler_params=small,
        name="payload",
    )(flux, *sent, *[hbm(x.reshape(pairs)) for x in (routes, dest_row, weight_id)], from_south, from_north)

    strip = shape_of((HALO_ROWS + ADJ_ROWS, LANES))
    to_east, to_west = pl.pallas_call(
        strip_kernel,
        out_shape=(strip, strip),
        in_specs=[vmem()] * 4,
        out_specs=(vmem(),) * 2,
        compiler_params=pltpu.CompilerParams(vmem_limit_bytes=8 << 20),
        name="strips",
    )(own_east, own_west, from_south, from_north)
    cols_up = [(c * 16 + i, c * 16 + (i + 1) % 16) for c in range(3) for i in range(16)]
    from_west = lax.ppermute(to_east, ("comp", "lon"), cols_up)
    from_east = lax.ppermute(to_west, ("comp", "lon"), [(b, a) for a, b in cols_up])

    gathered = lax.all_to_all(payload, ("lat", "lon"), split_axis=0, concat_axis=0, tiled=True)
    gathered = gathered.reshape(TILES * 40, LANES)

    spread_own, widen = spread_tables()
    wide = (ADJ_ROWS, WIDE)
    result = pl.pallas_call(
        ocean_kernel,
        out_shape=pltpu.HBM((FLD, LEVB, ROWS, COLS), f32),
        in_specs=[in_hbm()] * 8 + [vmem()] * 5,
        out_specs=in_hbm(),
        scratch_shapes=[
            SM((FLD,), f32),
            SM((FLD,), f32),
            SM((4, 8), f32),
            VM((LANES, 8 * COLS), bf16),
            VM((512, 512), bf16),
            VM((ROWS, COLS), jnp.int32),
            VM((2, PLANES, HALO_ROWS, WIDE), f32),
            VM((FLD, LEVB) + wide, f32),
            VM((HALO_ROWS, WIDE), f32),
            VM(wide, f32),
            VM((NSTEP, LEVB) + wide, f32),
            VM((NSTEP, LEVB) + wide, f32),
            VM((NSTEP, FLD, LEVB) + wide, f32),
            VM((NSTEP, FLD, LEVB) + wide, f32),
            VM((4 * ADJ_ROWS, 1024), bf16),
            VM((4 * ADJ_ROWS, 1024), bf16),
            VM((LANES, LANES), f32),
            VM((4, LANES, LANES), f32),
            VM((8, 4, ADJ_ROWS, LANES), f32),
            VM((2, 16 * TILES, LANES), f32),
            VM((TILES, COLS), f32),
            VM((1024, COLS), bf16),
            VM((1024, COLS), bf16),
            held,
            pltpu.SemaphoreType.DMA((6 + 2 * PLANES,)),
        ],
        compiler_params=pltpu.CompilerParams(vmem_limit_bytes=48 << 20),
        name="ocean",
    )(
        *[hbm(x) for x in (diffusivity, penetration, regrid_table.T, widen, spread_own)],
        mask_at,
        state_at,
        adj_at,
        from_south,
        from_north,
        from_west,
        from_east,
        gathered,
    )
    return result[None]


def solution(mesh):
    in_specs = (
        P("comp", None, None, "lat", "lon"),
        P("comp", None, None, "lat", "lon"),
        P("lat", "lon"),
        P(),
        P(),
        P(),
        P(("lat", "lon"), None),
        P(("lat", "lon")),
        P(("lat", "lon")),
        P(),
    )
    out_specs = P("comp", None, None, "lat", "lon")
    return jax.shard_map(shards, mesh=mesh, in_specs=in_specs, out_specs=out_specs, check_vma=False)
```

time: 71 us -> 71.5 us (level)
  the two profiles are of different devices: /device:TPU:1 before, /device:TPU:65 now
where the time goes in v2:
time: 71.5 us; the launch traced here: 71.1 us
  Pallas kernels  24.6 us (34%)
  starting transfers between devices  24.6 us (34%)
  waiting for transfers between devices  21.8 us (30%)
    pallas_call x1, Pallas kernels, shards(): pl.pallas_call(ocean_kernel, out_shape=pltpu.HBM((FLD, LEVB, ROWS, COLS),...  20.2 us
    all_to_all x1, starting transfers between devices, shards(): lax.all_to_all(payload, ('lat', 'lon'), split_axis=0, concat_axis=0, tile...  12.1 us
    all_to_all x1, waiting for transfers between devices, shards(): lax.all_to_all(payload, ('lat', 'lon'), split_axis=0, concat_axis=0, tile...  8.71 us
    ppermute x3, waiting for transfers between devices, shards(): sent = [lax.ppermute(flux, 'comp', [(3, band)]) for band in range(3)]  6.46 us
    ppermute x1, waiting for transfers between devices, shards(): from_west = lax.ppermute(to_east, ('comp', 'lon'), cols_up)  5.37 us
    ppermute x1, starting transfers between devices, shards(): from_west = lax.ppermute(to_east, ('comp', 'lon'), cols_up)  3.54 us
    ppermute x1, starting transfers between devices, shards(): from_south = lax.ppermute(to_north, ('comp', 'lat'), rows_up)  3.12 us
    ppermute x3, starting transfers between devices, shards(): sent = [lax.ppermute(flux, 'comp', [(3, band)]) for band in range(3)]  2.62 us
  transfers between devices with their start and end apart: 8, of which 4 were waited for; matrix products, arithmetic and copies ran while one was open for 0% of the time, Pallas kernels for 0%

profile of v2, /device:TPU:65, one launch (start us, length us, event | category | flops | bytes accessed | tf_op | source)
XLA Modules:
  0.0 71.1 jit_solution(8811036092784453964)
XLA Ops:
  0.0 1.9 %flux.1 = (f32[40,128]{1,0:T(8,128)S(1)}, f32[19,8,256]{2,1,0:T(8,128)S(1)}, f32[19,8,256]{2,1,0:T(8,128)S(1)}, f32[2,64,128]{2,1,0:T(8,128)S(1)}, f32[2,64,128]{2,1,0:T(8,128)S(1)}) custom-call(f32[6,2,64,256]{3,2,1,0:T(8,128)} %bitcast.9, f32[6,2,64,256]{3,2,1,0:T(8,128)} %bitcast.11, s32[64,256]{1,0:T(8,128)} %mask.3, f32[4,192]{1,0:T(4,128)} %weight.1), custom_call_target="tpu_custom_call" | custom-call | tf_op jit(solution)/shard_map/flux/pallas_call | solution.py:523
  1.9 3.1 %collective-permute-start = (f32[19,8,256]{2,1,0:T(8,128)S(1)}, f32[19,8,256]{2,1,0:T(8,128)S(1)}, u32[]{:S(2)}, u32[]{:S(2)}) collective-permute-start(f32[19,8,256]{2,1,0:T(8,128)S(1)} %get-tuple-element.12), channel_id=1, source_target_pairs={{0,16},{16,32},{32,48},{64,80},{80,96},{96,112},{128,144},{144,160... | collective-permute-start | bytes 466952 | tf_op jit(solution)/shard_map/ppermute | solution.py:545
  5.0 1.3 %collective-permute-start.1 = (f32[19,8,256]{2,1,0:T(8,128)S(1)}, f32[19,8,256]{2,1,0:T(8,128)S(1)}, u32[]{:S(2)}, u32[]{:S(2)}) collective-permute-start(f32[19,8,256]{2,1,0:T(8,128)S(1)} %get-tuple-element.13), channel_id=1, source_target_pairs={{16,0},{32,16},{48,32},{80,64},{96,80},{112,96},{144,128},{160,144... | collective-permute-start | bytes 466952 | tf_op jit(solution)/shard_map/ppermute | solution.py:546
  6.3 0.7 collective-permute-start.4
  7.0 1.3 %collective-permute-start.5 = (f32[40,128]{1,0:T(8,128)S(1)}, f32[40,128]{1,0:T(8,128)S(1)}, u32[]{:S(2)}, u32[]{:S(2)}) collective-permute-start(f32[40,128]{1,0:T(8,128)S(1)} %get-tuple-element.18.flux), channel_id=1, source_target_pairs={{192,64},{193,65},{194,66},{195,67},{196,68},{197,69},{198,70},{19... | collective-permute-start | bytes 61448 | tf_op jit(solution)/shard_map/ppermute | solution.py:543
  8.3 0.7 collective-permute-start.6
  9.0 0.0 collective-permute-done.4.first
  9.0 6.5 %collective-permute-done.5.second = f32[40,128]{1,0:T(8,128)S(1)} collective-permute-done((f32[40,128]{1,0:T(8,128)S(1)}, f32[40,128]{1,0:T(8,128)S(1)}, u32[]{:S(2)}, u32[]{:S(2)}) %collective-permute-start.5) | collective-permute-done | bytes 20512 | tf_op jit(solution)/shard_map/ppermute | solution.py:543
  15.4 0.0 collective-permute-done.6.third
  15.4 0.0 collective-permute-done.from_south.south
  15.4 0.0 collective-permute-done.1.from_north.north
  15.4 2.4 %payload.1 = f32[64,40,128]{2,1,0:T(8,128)} custom-call(f32[40,128]{1,0:T(8,128)S(1)} %get-tuple-element.18.flux, f32[40,128]{1,0:T(8,128)S(1)} %collective-permute-done.4.first, f32[40,128]{1,0:T(8,128)S(1)} %collective-permute-done.5.second, f32[40,128]{1,0:T(8,128)S(1)} %collective-permute-done.6.third, s32[2,128]{1,0:T(2,128)} %bitcast.14, ...), custom_call_target="tpu_custom_call" | custom-call | tf_op jit(solution)/shard_map/payload/pallas_call | solution.py:548
  17.8 12.1 %all-to-all-start = ((f32[64,40,128]{2,1,0:T(8,128)}), f32[64,40,128]{2,1,0:T(8,128)S(1)}, u32[]{:S(2)}, u32[]{:S(2)}) async-start(f32[64,40,128]{2,1,0:T(8,128)} %payload.1), calls=%async_computation | async-start | bytes 2621440 | tf_op jit(solution)/shard_map/all_to_all | solution.py:571
  30.0 0.1 strips.1
  30.1 3.5 %collective-permute-start.2 = (f32[152,128]{1,0:T(8,128)S(1)}, f32[152,128]{1,0:T(8,128)S(1)}, u32[]{:S(2)}, u32[]{:S(2)}) collective-permute-start(f32[152,128]{1,0:T(8,128)S(1)} %get-tuple-element.16), channel_id=1, source_target_pairs={{0,1},{1,2},{2,3},{3,4},{4,5},{5,6},{6,7},{7,8},{8,9},{9,10},{10,1... | collective-permute-start | bytes 233480 | tf_op jit(solution)/shard_map/ppermute | solution.py:568
  33.6 1.9 %collective-permute-start.3 = (f32[152,128]{1,0:T(8,128)S(1)}, f32[152,128]{1,0:T(8,128)S(1)}, u32[]{:S(2)}, u32[]{:S(2)}) collective-permute-start(f32[152,128]{1,0:T(8,128)S(1)} %get-tuple-element.17), channel_id=1, source_target_pairs={{1,0},{2,1},{3,2},{4,3},{5,4},{6,5},{7,6},{8,7},{9,8},{10,9},{11,1... | collective-permute-start | bytes 233480 | tf_op jit(solution)/shard_map/ppermute | solution.py:569
  35.6 5.4 %collective-permute-done.2.from_west = f32[152,128]{1,0:T(8,128)S(1)} collective-permute-done((f32[152,128]{1,0:T(8,128)S(1)}, f32[152,128]{1,0:T(8,128)S(1)}, u32[]{:S(2)}, u32[]{:S(2)}) %collective-permute-start.2) | collective-permute-done | bytes 77856 | tf_op jit(solution)/shard_map/ppermute | solution.py:568
  41.0 1.3 %collective-permute-done.3.from_east = f32[152,128]{1,0:T(8,128)S(1)} collective-permute-done((f32[152,128]{1,0:T(8,128)S(1)}, f32[152,128]{1,0:T(8,128)S(1)}, u32[]{:S(2)}, u32[]{:S(2)}) %collective-permute-start.3) | collective-permute-done | bytes 77856 | tf_op jit(solution)/shard_map/ppermute | solution.py:569
  42.2 8.7 %all-to-all-done = f32[64,40,128]{2,1,0:T(8,128)S(1)} async-done(((f32[64,40,128]{2,1,0:T(8,128)}), f32[64,40,128]{2,1,0:T(8,128)S(1)}, u32[]{:S(2)}, u32[]{:S(2)}) %all-to-all-start) | async-done | bytes 1310752 | tf_op jit(solution)/shard_map/all_to_all | solution.py:571
  50.9 20.2 %ocean.1 = f32[6,2,64,256]{3,2,1,0:T(8,128)} custom-call(f32[6]{0:T(128)} %diffusivity_at.1, f32[6]{0:T(128)} %penetration_at.1, f32[4,8]{1,0:T(4,128)} %bitcast.13, bf16[128,2048]{1,0:T(8,128)(2,1)} %constant.4.clone.widen_at, bf16[512,512]{1,0:T(8,128)(2,1)} %constant.5.clone.spread_own_at, s32[64,256]{1,0:T(8,128)} %mask.3, f32[6,2,64,256]{3,2,1,0:T(8,128)} %bitcast.10, ...), custom_call_target="tpu_custom_call" | custom-call | tf_op jit(solution)/shard_map/ocean/pallas_call | solution.py:576
Async XLA Ops:
  1.9 13.5 %collective-permute-start = (f32[19,8,256]{2,1,0:T(8,128)S(1)}, f32[19,8,256]{2,1,0:T(8,128)S(1)}, u32[]{:S(2)}, u32[]{:S(2)}) collective-permute-start(f32[19,8,256]{2,1,0:T(8,128)S(1)} %get-tuple-element.12), channel_id=1, source_target_pairs={{0,16},{16,32},{32,48},{64,80},{80,96},{96,112},{128,144},{144,160... | collective-permute-start | bytes 466952 | tf_op jit(solution)/shard_map/ppermute | solution.py:545
  5.0 10.4 %collective-permute-start.1 = (f32[19,8,256]{2,1,0:T(8,128)S(1)}, f32[19,8,256]{2,1,0:T(8,128)S(1)}, u32[]{:S(2)}, u32[]{:S(2)}) collective-permute-start(f32[19,8,256]{2,1,0:T(8,128)S(1)} %get-tuple-element.13), channel_id=1, source_target_pairs={{16,0},{32,16},{48,32},{80,64},{96,80},{112,96},{144,128},{160,144... | collective-permute-start | bytes 466952 | tf_op jit(solution)/shard_map/ppermute | solution.py:546
  6.3 2.6 %collective-permute-start.4 = (f32[40,128]{1,0:T(8,128)S(1)}, f32[40,128]{1,0:T(8,128)S(1)}, u32[]{:S(2)}, u32[]{:S(2)}) collective-permute-start(f32[40,128]{1,0:T(8,128)S(1)} %get-tuple-element.18.flux), channel_id=1, source_target_pairs={{192,0},{193,1},{194,2},{195,3},{196,4},{197,5},{198,6},{199,7},{2... | collective-permute-start | bytes 61448 | tf_op jit(solution)/shard_map/ppermute | solution.py:543
  7.0 8.4 %collective-permute-start.5 = (f32[40,128]{1,0:T(8,128)S(1)}, f32[40,128]{1,0:T(8,128)S(1)}, u32[]{:S(2)}, u32[]{:S(2)}) collective-permute-start(f32[40,128]{1,0:T(8,128)S(1)} %get-tuple-element.18.flux), channel_id=1, source_target_pairs={{192,64},{193,65},{194,66},{195,67},{196,68},{197,69},{198,70},{19... | collective-permute-start | bytes 61448 | tf_op jit(solution)/shard_map/ppermute | solution.py:543
  8.3 7.1 %collective-permute-start.6 = (f32[40,128]{1,0:T(8,128)S(1)}, f32[40,128]{1,0:T(8,128)S(1)}, u32[]{:S(2)}, u32[]{:S(2)}) collective-permute-start(f32[40,128]{1,0:T(8,128)S(1)} %get-tuple-element.18.flux), channel_id=1, source_target_pairs={{192,128},{193,129},{194,130},{195,131},{196,132},{197,133},{198,1... | collective-permute-start | bytes 61448 | tf_op jit(solution)/shard_map/ppermute | solution.py:543
  17.8 33.1 %all-to-all-start = ((f32[64,40,128]{2,1,0:T(8,128)}), f32[64,40,128]{2,1,0:T(8,128)S(1)}, u32[]{:S(2)}, u32[]{:S(2)}) async-start(f32[64,40,128]{2,1,0:T(8,128)} %payload.1), calls=%async_computation | async-start | bytes 2621440 | tf_op jit(solution)/shard_map/all_to_all | solution.py:571
  30.1 10.8 %collective-permute-start.2 = (f32[152,128]{1,0:T(8,128)S(1)}, f32[152,128]{1,0:T(8,128)S(1)}, u32[]{:S(2)}, u32[]{:S(2)}) collective-permute-start(f32[152,128]{1,0:T(8,128)S(1)} %get-tuple-element.16), channel_id=1, source_target_pairs={{0,1},{1,2},{2,3},{3,4},{4,5},{5,6},{6,7},{7,8},{8,9},{9,10},{10,1... | collective-permute-start | bytes 233480 | tf_op jit(solution)/shard_map/ppermute | solution.py:568
  33.6 8.6 %collective-permute-start.3 = (f32[152,128]{1,0:T(8,128)S(1)}, f32[152,128]{1,0:T(8,128)S(1)}, u32[]{:S(2)}, u32[]{:S(2)}) collective-permute-start(f32[152,128]{1,0:T(8,128)S(1)} %get-tuple-element.17), channel_id=1, source_target_pairs={{1,0},{2,1},{3,2},{4,3},{5,4},{6,5},{7,6},{8,7},{9,8},{10,9},{11,1... | collective-permute-start | bytes 233480 | tf_op jit(solution)/shard_map/ppermute | solution.py:569

commit v3 on v2

--- a/solution.py
+++ b/solution.py
@@ -104,6 +104,9 @@
     adjoint_in,
     mask,
     weight,
+    routes,
+    dest_row,
+    weight_id,
     flux,
     to_north,
     to_south,
@@ -113,8 +116,16 @@
     held_adj,
     held_mask,
     held_weight,
+    lists,
     sems,
 ):
+    listing = [
+        pltpu.make_async_copy(x, lists.at[pl.ds(2 * at, 2)], sems.at[4 + at])
+        for at, x in enumerate((routes, dest_row, weight_id))
+    ]
+    for copy in listing:
+        copy.start()
+    flux[40:, :] = jnp.zeros((flux.shape[0] - 40, LANES), f32)
     pairs = ((checkpoint, held), (adjoint_in, held_adj), (mask, held_mask), (weight, held_weight))
     copies = [pltpu.make_async_copy(source, target, sems.at[at]) for at, (source, target) in enumerate(pairs)]
     for copy in copies:
@@ -122,7 +133,11 @@
 
     @pl.when(lax.axis_index("comp") != 3)
     def _():
-        flux[...] = jnp.zeros((40, LANES), f32)
+        flux[0:33, :] = jnp.zeros((33, LANES), f32)
+        for copy in listing:
+            copy.wait()
+        flux[33:39, :] = lists[0:6, :].astype(f32)
+        flux[39:40, :] = jnp.zeros((1, LANES), f32)
         for copy in copies:
             copy.wait()
         top, low = slice(ROWS - 8, ROWS), slice(0, 8)
@@ -145,6 +160,8 @@
 
     @pl.when(lax.axis_index("comp") == 3)
     def _():
+        for copy in listing:
+            copy.wait()
         copies[3].wait()
         w = held_weight[...]
         parts = jnp.concatenate(exact_parts(w) + [jnp.zeros_like(w)], axis=0).astype(bf16)
@@ -197,18 +214,9 @@
         to_east[rows, :], to_west[rows, :] = packed_strips([x[:, 0:LANES] for x in planes], [x[:, LANES:] for x in planes])
 
 
-def payload_kernel(flux, first, second, third, routes, dest_row, weight_id, south, north, payload, block, lists, sems):
+def payload_kernel(flux, first, second, third, south, north, payload, block, sems):
     del south, north
-    copies = [
-        pltpu.make_async_copy(x, lists.at[pl.ds(2 * at, 2)], sems.at[at])
-        for at, x in enumerate((routes, dest_row, weight_id))
-    ]
-    for copy in copies:
-        copy.start()
-    block[...] = flux[...] + (first[...] + second[...] + third[...])
-    for copy in copies:
-        copy.wait()
-    block[33:39, :] = lists[0:6, :].astype(f32)
+    block[...] = flux[0:40, :] + (first[0:40, :] + second[0:40, :] + third[0:40, :])
     copies = [pltpu.make_async_copy(block, payload.at[tile], sems.at[tile]) for tile in range(TILES)]
     for copy in copies:
         copy.start()
@@ -522,15 +530,16 @@
     small = pltpu.CompilerParams(vmem_limit_bytes=2 << 20)
     flux, to_north, to_south, own_east, own_west = pl.pallas_call(
         flux_kernel,
-        out_shape=(shape_of((40, LANES)), edge, edge, own_strip, own_strip),
-        in_specs=[in_hbm()] * 4,
+        out_shape=(shape_of((312, LANES)), edge, edge, own_strip, own_strip),
+        in_specs=[in_hbm()] * 7,
         out_specs=(vmem(),) * 5,
         scratch_shapes=[
             held,
             held,
             VM((ROWS, COLS), jnp.int32),
             VM((NFLUX, FLD * 32), f32),
-            pltpu.SemaphoreType.DMA((4,)),
+            VM((8, LANES), jnp.int32),
+            pltpu.SemaphoreType.DMA((7,)),
         ],
         compiler_params=pltpu.CompilerParams(vmem_limit_bytes=12 << 20),
         name="flux",
@@ -538,7 +547,7 @@
         state_at,
         adj_at,
         mask_at,
-        hbm(column_weight),
+        *[hbm(x) for x in (column_weight, routes.reshape(pairs), dest_row.reshape(pairs), weight_id.reshape(pairs))],
     )
     sent = [lax.ppermute(flux, "comp", [(3, band)]) for band in range(3)]
     rows_up = [(c * 4 + i, c * 4 + i + 1) for c in range(3) for i in range(3)]
@@ -548,12 +557,12 @@
     payload = pl.pallas_call(
         payload_kernel,
         out_shape=pltpu.HBM((TILES, 40, LANES), f32),
-        in_specs=[vmem()] * 4 + [in_hbm()] * 3 + [any_place] * 2,
+        in_specs=[vmem()] * 4 + [any_place] * 2,
         out_specs=in_hbm(),
-        scratch_shapes=[VM((40, LANES), f32), VM((8, LANES), jnp.int32), pltpu.SemaphoreType.DMA((TILES,))],
+        scratch_shapes=[VM((40, LANES), f32), pltpu.SemaphoreType.DMA((TILES,))],
         compiler_params=small,
         name="payload",
-    )(flux, *sent, *[hbm(x.reshape(pairs)) for x in (routes, dest_row, weight_id)], from_south, from_north)
+    )(flux, *sent, from_south, from_north)
 
     strip = shape_of((HALO_ROWS + ADJ_ROWS, LANES))
     to_east, to_west = pl.pallas_call(

time: 71.5 us -> 73.4 us (1.027)
  the two profiles are of different devices: /device:TPU:65 before, /device:TPU:1 now
where the time goes in v3:
time: 73.4 us; the launch traced here: 73.1 us
  starting transfers between devices  28.5 us (39%)
  Pallas kernels  24 us (33%)
  waiting for transfers between devices  20.5 us (28%)
    pallas_call x1, Pallas kernels, shards(): pl.pallas_call(ocean_kernel, out_shape=pltpu.HBM((FLD, LEVB, ROWS, COLS),...  20.2 us
    all_to_all x1, starting transfers between devices, shards(): lax.all_to_all(payload, ('lat', 'lon'), split_axis=0, concat_axis=0, tile...  15.1 us
    all_to_all x1, waiting for transfers between devices, shards(): lax.all_to_all(payload, ('lat', 'lon'), split_axis=0, concat_axis=0, tile...  8.71 us
    ppermute x1, waiting for transfers between devices, shards(): from_west = lax.ppermute(to_east, ('comp', 'lon'), cols_up)  5.37 us
    ppermute x1, starting transfers between devices, shards(): from_south = lax.ppermute(to_north, ('comp', 'lat'), rows_up)  3.95 us
    ppermute x1, waiting for transfers between devices, shards(): lax.ppermute(to_south, ('comp', 'lat'), [(b, a) for a, b in rows_up])  3.8 us
    ppermute x1, starting transfers between devices, shards(): from_west = lax.ppermute(to_east, ('comp', 'lon'), cols_up)  3.54 us
    ppermute x3, starting transfers between devices, shards(): sent = [lax.ppermute(flux, 'comp', [(3, band)]) for band in range(3)]  2.63 us
  transfers between devices with their start and end apart: 8, of which 5 were waited for; matrix products, arithmetic and copies ran while one was open for 0% of the time, Pallas kernels for 0%

profile of v3, /device:TPU:1, one launch (start us, length us, event | category | flops | bytes accessed | tf_op | source)
XLA Modules:
  0.0 73.1 jit_solution(8219324915827513362)
XLA Ops:
  0.0 2.0 %flux.1 = (f32[312,128]{1,0:T(8,128)S(1)}, f32[19,8,256]{2,1,0:T(8,128)S(1)}, f32[19,8,256]{2,1,0:T(8,128)S(1)}, f32[2,64,128]{2,1,0:T(8,128)S(1)}, f32[2,64,128]{2,1,0:T(8,128)S(1)}) custom-call(f32[6,2,64,256]{3,2,1,0:T(8,128)} %bitcast.9, f32[6,2,64,256]{3,2,1,0:T(8,128)} %bitcast.11, s32[64,256]{1,0:T(8,128)} %mask.3, f32[4,192]{1,0:T(4,128)} %weight.1, ...), custom_call_target="tpu_custom_call" | custom-call | tf_op jit(solution)/shard_map/flux/pallas_call | solution.py:531
  2.0 1.3 %collective-permute-start.4 = (f32[312,128]{1,0:T(8,128)S(1)}, f32[312,128]{1,0:T(8,128)S(1)}, u32[]{:S(2)}, u32[]{:S(2)}) collective-permute-start(f32[312,128]{1,0:T(8,128)S(1)} %get-tuple-element.18.flux), channel_id=1, source_target_pairs={{192,0},{193,1},{194,2},{195,3},{196,4},{197,5},{198,6},{199,7},{2... | collective-permute-start | bytes 479240 | tf_op jit(solution)/shard_map/ppermute | solution.py:552
  3.3 0.7 collective-permute-start.5
  4.0 0.7 collective-permute-start.6
  4.6 4.0 %collective-permute-start = (f32[19,8,256]{2,1,0:T(8,128)S(1)}, f32[19,8,256]{2,1,0:T(8,128)S(1)}, u32[]{:S(2)}, u32[]{:S(2)}) collective-permute-start(f32[19,8,256]{2,1,0:T(8,128)S(1)} %get-tuple-element.12), channel_id=1, source_target_pairs={{0,16},{16,32},{32,48},{64,80},{80,96},{96,112},{128,144},{144,160... | collective-permute-start | bytes 466952 | tf_op jit(solution)/shard_map/ppermute | solution.py:554
  8.6 1.3 %collective-permute-start.1 = (f32[19,8,256]{2,1,0:T(8,128)S(1)}, f32[19,8,256]{2,1,0:T(8,128)S(1)}, u32[]{:S(2)}, u32[]{:S(2)}) collective-permute-start(f32[19,8,256]{2,1,0:T(8,128)S(1)} %get-tuple-element.13), channel_id=1, source_target_pairs={{16,0},{32,16},{48,32},{80,64},{96,80},{112,96},{144,128},{160,144... | collective-permute-start | bytes 466952 | tf_op jit(solution)/shard_map/ppermute | solution.py:555
  9.9 1.4 %collective-permute-done.from_south.south = f32[19,8,256]{2,1,0:T(8,128)S(1)} collective-permute-done((f32[19,8,256]{2,1,0:T(8,128)S(1)}, f32[19,8,256]{2,1,0:T(8,128)S(1)}, u32[]{:S(2)}, u32[]{:S(2)}) %collective-permute-start) | collective-permute-done | bytes 155680 | tf_op jit(solution)/shard_map/ppermute | solution.py:554
  11.3 3.8 %collective-permute-done.1.from_north.north = f32[19,8,256]{2,1,0:T(8,128)S(1)} collective-permute-done((f32[19,8,256]{2,1,0:T(8,128)S(1)}, f32[19,8,256]{2,1,0:T(8,128)S(1)}, u32[]{:S(2)}, u32[]{:S(2)}) %collective-permute-start.1) | collective-permute-done | bytes 155680 | tf_op jit(solution)/shard_map/ppermute | solution.py:555
  15.1 0.0 collective-permute-done.4.first
  15.1 0.0 collective-permute-done.5.second
  15.1 0.0 collective-permute-done.6.third
  15.1 1.7 %payload.1 = f32[64,40,128]{2,1,0:T(8,128)} custom-call(f32[312,128]{1,0:T(8,128)S(1)} %get-tuple-element.18.flux, f32[312,128]{1,0:T(8,128)S(1)} %collective-permute-done.4.first, f32[312,128]{1,0:T(8,128)S(1)} %collective-permute-done.5.second, f32[312,128]{1,0:T(8,128)S(1)} %collective-permute-done.6.third, ...), custom_call_target="tpu_custom_call" | custom-call | tf_op jit(solution)/shard_map/payload/pallas_call | solution.py:557
  16.8 15.1 %all-to-all-start = ((f32[64,40,128]{2,1,0:T(8,128)}), f32[64,40,128]{2,1,0:T(8,128)S(1)}, u32[]{:S(2)}, u32[]{:S(2)}) async-start(f32[64,40,128]{2,1,0:T(8,128)} %payload.1), calls=%async_computation | async-start | bytes 2621440 | tf_op jit(solution)/shard_map/all_to_all | solution.py:580
  31.9 0.1 strips.1
  32.0 3.5 %collective-permute-start.2 = (f32[152,128]{1,0:T(8,128)S(1)}, f32[152,128]{1,0:T(8,128)S(1)}, u32[]{:S(2)}, u32[]{:S(2)}) collective-permute-start(f32[152,128]{1,0:T(8,128)S(1)} %get-tuple-element.16), channel_id=1, source_target_pairs={{0,1},{1,2},{2,3},{3,4},{4,5},{5,6},{6,7},{7,8},{8,9},{9,10},{10,1... | collective-permute-start | bytes 233480 | tf_op jit(solution)/shard_map/ppermute | solution.py:577
  35.6 1.9 %collective-permute-start.3 = (f32[152,128]{1,0:T(8,128)S(1)}, f32[152,128]{1,0:T(8,128)S(1)}, u32[]{:S(2)}, u32[]{:S(2)}) collective-permute-start(f32[152,128]{1,0:T(8,128)S(1)} %get-tuple-element.17), channel_id=1, source_target_pairs={{1,0},{2,1},{3,2},{4,3},{5,4},{6,5},{7,6},{8,7},{9,8},{10,9},{11,1... | collective-permute-start | bytes 233480 | tf_op jit(solution)/shard_map/ppermute | solution.py:578
  37.5 5.4 %collective-permute-done.2.from_west = f32[152,128]{1,0:T(8,128)S(1)} collective-permute-done((f32[152,128]{1,0:T(8,128)S(1)}, f32[152,128]{1,0:T(8,128)S(1)}, u32[]{:S(2)}, u32[]{:S(2)}) %collective-permute-start.2) | collective-permute-done | bytes 77856 | tf_op jit(solution)/shard_map/ppermute | solution.py:577
  42.9 1.3 %collective-permute-done.3.from_east = f32[152,128]{1,0:T(8,128)S(1)} collective-permute-done((f32[152,128]{1,0:T(8,128)S(1)}, f32[152,128]{1,0:T(8,128)S(1)}, u32[]{:S(2)}, u32[]{:S(2)}) %collective-permute-start.3) | collective-permute-done | bytes 77856 | tf_op jit(solution)/shard_map/ppermute | solution.py:578
  44.1 8.7 %all-to-all-done = f32[64,40,128]{2,1,0:T(8,128)S(1)} async-done(((f32[64,40,128]{2,1,0:T(8,128)}), f32[64,40,128]{2,1,0:T(8,128)S(1)}, u32[]{:S(2)}, u32[]{:S(2)}) %all-to-all-start) | async-done | bytes 1310752 | tf_op jit(solution)/shard_map/all_to_all | solution.py:580
  52.9 20.2 %ocean.1 = f32[6,2,64,256]{3,2,1,0:T(8,128)} custom-call(f32[6]{0:T(128)} %diffusivity_at.1, f32[6]{0:T(128)} %penetration_at.1, f32[4,8]{1,0:T(4,128)} %bitcast.13, bf16[128,2048]{1,0:T(8,128)(2,1)} %constant.4.clone.widen_at, bf16[512,512]{1,0:T(8,128)(2,1)} %constant.5.clone.spread_own_at, s32[64,256]{1,0:T(8,128)} %mask.3, f32[6,2,64,256]{3,2,1,0:T(8,128)} %bitcast.10, ...), custom_call_target="tpu_custom_call" | custom-call | tf_op jit(solution)/shard_map/ocean/pallas_call | solution.py:585
Async XLA Ops:
  2.0 13.1 %collective-permute-start.4 = (f32[312,128]{1,0:T(8,128)S(1)}, f32[312,128]{1,0:T(8,128)S(1)}, u32[]{:S(2)}, u32[]{:S(2)}) collective-permute-start(f32[312,128]{1,0:T(8,128)S(1)} %get-tuple-element.18.flux), channel_id=1, source_target_pairs={{192,0},{193,1},{194,2},{195,3},{196,4},{197,5},{198,6},{199,7},{2... | collective-permute-start | bytes 479240 | tf_op jit(solution)/shard_map/ppermute | solution.py:552
  3.3 11.8 %collective-permute-start.5 = (f32[312,128]{1,0:T(8,128)S(1)}, f32[312,128]{1,0:T(8,128)S(1)}, u32[]{:S(2)}, u32[]{:S(2)}) collective-permute-start(f32[312,128]{1,0:T(8,128)S(1)} %get-tuple-element.18.flux), channel_id=1, source_target_pairs={{192,64},{193,65},{194,66},{195,67},{196,68},{197,69},{198,70},{19... | collective-permute-start | bytes 479240 | tf_op jit(solution)/shard_map/ppermute | solution.py:552
  4.0 11.1 %collective-permute-start.6 = (f32[312,128]{1,0:T(8,128)S(1)}, f32[312,128]{1,0:T(8,128)S(1)}, u32[]{:S(2)}, u32[]{:S(2)}) collective-permute-start(f32[312,128]{1,0:T(8,128)S(1)} %get-tuple-element.18.flux), channel_id=1, source_target_pairs={{192,128},{193,129},{194,130},{195,131},{196,132},{197,133},{198,1... | collective-permute-start | bytes 479240 | tf_op jit(solution)/shard_map/ppermute | solution.py:552
  4.6 6.6 %collective-permute-start = (f32[19,8,256]{2,1,0:T(8,128)S(1)}, f32[19,8,256]{2,1,0:T(8,128)S(1)}, u32[]{:S(2)}, u32[]{:S(2)}) collective-permute-start(f32[19,8,256]{2,1,0:T(8,128)S(1)} %get-tuple-element.12), channel_id=1, source_target_pairs={{0,16},{16,32},{32,48},{64,80},{80,96},{96,112},{128,144},{144,160... | collective-permute-start | bytes 466952 | tf_op jit(solution)/shard_map/ppermute | solution.py:554
  8.6 6.5 %collective-permute-start.1 = (f32[19,8,256]{2,1,0:T(8,128)S(1)}, f32[19,8,256]{2,1,0:T(8,128)S(1)}, u32[]{:S(2)}, u32[]{:S(2)}) collective-permute-start(f32[19,8,256]{2,1,0:T(8,128)S(1)} %get-tuple-element.13), channel_id=1, source_target_pairs={{16,0},{32,16},{48,32},{80,64},{96,80},{112,96},{144,128},{160,144... | collective-permute-start | bytes 466952 | tf_op jit(solution)/shard_map/ppermute | solution.py:555
  16.8 36.1 %all-to-all-start = ((f32[64,40,128]{2,1,0:T(8,128)}), f32[64,40,128]{2,1,0:T(8,128)S(1)}, u32[]{:S(2)}, u32[]{:S(2)}) async-start(f32[64,40,128]{2,1,0:T(8,128)} %payload.1), calls=%async_computation | async-start | bytes 2621440 | tf_op jit(solution)/shard_map/all_to_all | solution.py:580
  32.0 10.8 %collective-permute-start.2 = (f32[152,128]{1,0:T(8,128)S(1)}, f32[152,128]{1,0:T(8,128)S(1)}, u32[]{:S(2)}, u32[]{:S(2)}) collective-permute-start(f32[152,128]{1,0:T(8,128)S(1)} %get-tuple-element.16), channel_id=1, source_target_pairs={{0,1},{1,2},{2,3},{3,4},{4,5},{5,6},{6,7},{7,8},{8,9},{9,10},{10,1... | collective-permute-start | bytes 233480 | tf_op jit(solution)/shard_map/ppermute | solution.py:577
  35.6 8.6 %collective-permute-start.3 = (f32[152,128]{1,0:T(8,128)S(1)}, f32[152,128]{1,0:T(8,128)S(1)}, u32[]{:S(2)}, u32[]{:S(2)}) collective-permute-start(f32[152,128]{1,0:T(8,128)S(1)} %get-tuple-element.17), channel_id=1, source_target_pairs={{1,0},{2,1},{3,2},{4,3},{5,4},{6,5},{7,6},{8,7},{9,8},{10,9},{11,1... | collective-permute-start | bytes 233480 | tf_op jit(solution)/shard_map/ppermute | solution.py:578

commit v4 on v3

--- a/solution.py
+++ b/solution.py
@@ -125,7 +125,6 @@
     ]
     for copy in listing:
         copy.start()
-    flux[40:, :] = jnp.zeros((flux.shape[0] - 40, LANES), f32)
     pairs = ((checkpoint, held), (adjoint_in, held_adj), (mask, held_mask), (weight, held_weight))
     copies = [pltpu.make_async_copy(source, target, sems.at[at]) for at, (source, target) in enumerate(pairs)]
     for copy in copies:
@@ -530,7 +529,7 @@
     small = pltpu.CompilerParams(vmem_limit_bytes=2 << 20)
     flux, to_north, to_south, own_east, own_west = pl.pallas_call(
         flux_kernel,
-        out_shape=(shape_of((312, LANES)), edge, edge, own_strip, own_strip),
+        out_shape=(shape_of((40, LANES)), edge, edge, own_strip, own_strip),
         in_specs=[in_hbm()] * 7,
         out_specs=(vmem(),) * 5,
         scratch_shapes=[
@@ -549,7 +548,7 @@
         mask_at,
         *[hbm(x) for x in (column_weight, routes.reshape(pairs), dest_row.reshape(pairs), weight_id.reshape(pairs))],
     )
-    sent = [lax.ppermute(flux, "comp", [(3, band)]) for band in range(3)]
+    sent = [lax.ppermute(flux, "comp", [(3, band)]) for band in (1, 0, 2)]
     rows_up = [(c * 4 + i, c * 4 + i + 1) for c in range(3) for i in range(3)]
     from_south = lax.ppermute(to_north, ("comp", "lat"), rows_up)
     from_north = lax.ppermute(to_south, ("comp", "lat"), [(b, a) for a, b in rows_up])

time: 73.4 us -> 73.2 us (level)
  starting transfers between devices: 28.5 us -> 25.3 us
  waiting for transfers between devices: 20.5 us -> 23.4 us
    ppermute x3, waiting for transfers between devices: 0.01 us -> 8.1 us  [shards(): sent = [lax.ppermute(flux, 'comp', [(3, band)]) for band in (1, 0, 2)]]
    ppermute x1, waiting for transfers between devices: 3.8 us -> 0.01 us  [shards(): lax.ppermute(to_south, ('comp', 'lat'), [(b, a) for a, b in rows_up])]
    all_to_all x1, starting transfers between devices: 15.1 us -> 12 us  [shards(): lax.all_to_all(payload, ('lat', 'lon'), split_axis=0, concat_axis=0, tile...]
    ppermute x1, waiting for transfers between devices: 1.36 us -> 0.01 us  [shards(): from_south = lax.ppermute(to_north, ('comp', 'lat'), rows_up)]
  transfers between devices with their start and end apart: 8 -> 8, of which waited for: 5 -> 4; matrix products, arithmetic and copies ran while one was open for 0% -> 0% of each run, Pallas kernels for 0% -> 0%
where the time goes in v4:
time: 73.2 us; the launch traced here: 72.9 us
  starting transfers between devices  25.3 us (35%)
  Pallas kernels  24 us (33%)
  waiting for transfers between devices  23.4 us (32%)
    pallas_call x1, Pallas kernels, shards(): pl.pallas_call(ocean_kernel, out_shape=pltpu.HBM((FLD, LEVB, ROWS, COLS),...  20.2 us
    all_to_all x1, starting transfers between devices, shards(): lax.all_to_all(payload, ('lat', 'lon'), split_axis=0, concat_axis=0, tile...  12 us
    all_to_all x1, waiting for transfers between devices, shards(): lax.all_to_all(payload, ('lat', 'lon'), split_axis=0, concat_axis=0, tile...  8.71 us
    ppermute x3, waiting for transfers between devices, shards(): sent = [lax.ppermute(flux, 'comp', [(3, band)]) for band in (1, 0, 2)]  8.1 us
    ppermute x1, waiting for transfers between devices, shards(): from_west = lax.ppermute(to_east, ('comp', 'lon'), cols_up)  5.37 us
    ppermute x1, starting transfers between devices, shards(): from_south = lax.ppermute(to_north, ('comp', 'lat'), rows_up)  3.95 us
    ppermute x1, starting transfers between devices, shards(): from_west = lax.ppermute(to_east, ('comp', 'lon'), cols_up)  3.54 us
    ppermute x3, starting transfers between devices, shards(): sent = [lax.ppermute(flux, 'comp', [(3, band)]) for band in (1, 0, 2)]  2.62 us
  transfers between devices with their start and end apart: 8, of which 4 were waited for; matrix products, arithmetic and copies ran while one was open for 0% of the time, Pallas kernels for 0%

profile of v4, /device:TPU:1, one launch (start us, length us, event | category | flops | bytes accessed | tf_op | source)
XLA Modules:
  0.0 72.9 jit_solution(11478296302675671848)
XLA Ops:
  0.0 2.0 %flux.1 = (f32[40,128]{1,0:T(8,128)S(1)}, f32[19,8,256]{2,1,0:T(8,128)S(1)}, f32[19,8,256]{2,1,0:T(8,128)S(1)}, f32[2,64,128]{2,1,0:T(8,128)S(1)}, f32[2,64,128]{2,1,0:T(8,128)S(1)}) custom-call(f32[6,2,64,256]{3,2,1,0:T(8,128)} %bitcast.9, f32[6,2,64,256]{3,2,1,0:T(8,128)} %bitcast.11, s32[64,256]{1,0:T(8,128)} %mask.3, f32[4,192]{1,0:T(4,128)} %weight.1, ...), custom_call_target="tpu_custom_call" | custom-call | tf_op jit(solution)/shard_map/flux/pallas_call | solution.py:530
  2.0 4.0 %collective-permute-start = (f32[19,8,256]{2,1,0:T(8,128)S(1)}, f32[19,8,256]{2,1,0:T(8,128)S(1)}, u32[]{:S(2)}, u32[]{:S(2)}) collective-permute-start(f32[19,8,256]{2,1,0:T(8,128)S(1)} %get-tuple-element.12), channel_id=1, source_target_pairs={{0,16},{16,32},{32,48},{64,80},{80,96},{96,112},{128,144},{144,160... | collective-permute-start | bytes 466952 | tf_op jit(solution)/shard_map/ppermute | solution.py:553
  5.9 1.3 %collective-permute-start.1 = (f32[19,8,256]{2,1,0:T(8,128)S(1)}, f32[19,8,256]{2,1,0:T(8,128)S(1)}, u32[]{:S(2)}, u32[]{:S(2)}) collective-permute-start(f32[19,8,256]{2,1,0:T(8,128)S(1)} %get-tuple-element.13), channel_id=1, source_target_pairs={{16,0},{32,16},{48,32},{80,64},{96,80},{112,96},{144,128},{160,144... | collective-permute-start | bytes 466952 | tf_op jit(solution)/shard_map/ppermute | solution.py:554
  7.2 0.7 collective-permute-start.4
  7.9 1.3 %collective-permute-start.5 = (f32[40,128]{1,0:T(8,128)S(1)}, f32[40,128]{1,0:T(8,128)S(1)}, u32[]{:S(2)}, u32[]{:S(2)}) collective-permute-start(f32[40,128]{1,0:T(8,128)S(1)} %get-tuple-element.18.flux), channel_id=1, source_target_pairs={{192,0},{193,1},{194,2},{195,3},{196,4},{197,5},{198,6},{199,7},{2... | collective-permute-start | bytes 61448 | tf_op jit(solution)/shard_map/ppermute | solution.py:551
  9.2 0.7 collective-permute-start.6
  9.9 0.0 collective-permute-done.4.first
  9.9 8.1 %collective-permute-done.5.second = f32[40,128]{1,0:T(8,128)S(1)} collective-permute-done((f32[40,128]{1,0:T(8,128)S(1)}, f32[40,128]{1,0:T(8,128)S(1)}, u32[]{:S(2)}, u32[]{:S(2)}) %collective-permute-start.5) | collective-permute-done | bytes 20512 | tf_op jit(solution)/shard_map/ppermute | solution.py:551
  18.0 0.0 collective-permute-done.6.third
  18.0 0.0 collective-permute-done.from_south.south
  18.0 0.0 collective-permute-done.1.from_north.north
  18.0 1.7 %payload.1 = f32[64,40,128]{2,1,0:T(8,128)} custom-call(f32[40,128]{1,0:T(8,128)S(1)} %get-tuple-element.18.flux, f32[40,128]{1,0:T(8,128)S(1)} %collective-permute-done.4.first, f32[40,128]{1,0:T(8,128)S(1)} %collective-permute-done.5.second, f32[40,128]{1,0:T(8,128)S(1)} %collective-permute-done.6.third, ...), custom_call_target="tpu_custom_call" | custom-call | tf_op jit(solution)/shard_map/payload/pallas_call | solution.py:556
  19.7 12.0 %all-to-all-start = ((f32[64,40,128]{2,1,0:T(8,128)}), f32[64,40,128]{2,1,0:T(8,128)S(1)}, u32[]{:S(2)}, u32[]{:S(2)}) async-start(f32[64,40,128]{2,1,0:T(8,128)} %payload.1), calls=%async_computation | async-start | bytes 2621440 | tf_op jit(solution)/shard_map/all_to_all | solution.py:579
  31.7 0.1 strips.1
  31.8 3.5 %collective-permute-start.2 = (f32[152,128]{1,0:T(8,128)S(1)}, f32[152,128]{1,0:T(8,128)S(1)}, u32[]{:S(2)}, u32[]{:S(2)}) collective-permute-start(f32[152,128]{1,0:T(8,128)S(1)} %get-tuple-element.16), channel_id=1, source_target_pairs={{0,1},{1,2},{2,3},{3,4},{4,5},{5,6},{6,7},{7,8},{8,9},{9,10},{10,1... | collective-permute-start | bytes 233480 | tf_op jit(solution)/shard_map/ppermute | solution.py:576
  35.4 1.9 %collective-permute-start.3 = (f32[152,128]{1,0:T(8,128)S(1)}, f32[152,128]{1,0:T(8,128)S(1)}, u32[]{:S(2)}, u32[]{:S(2)}) collective-permute-start(f32[152,128]{1,0:T(8,128)S(1)} %get-tuple-element.17), channel_id=1, source_target_pairs={{1,0},{2,1},{3,2},{4,3},{5,4},{6,5},{7,6},{8,7},{9,8},{10,9},{11,1... | collective-permute-start | bytes 233480 | tf_op jit(solution)/shard_map/ppermute | solution.py:577
  37.3 5.4 %collective-permute-done.2.from_west = f32[152,128]{1,0:T(8,128)S(1)} collective-permute-done((f32[152,128]{1,0:T(8,128)S(1)}, f32[152,128]{1,0:T(8,128)S(1)}, u32[]{:S(2)}, u32[]{:S(2)}) %collective-permute-start.2) | collective-permute-done | bytes 77856 | tf_op jit(solution)/shard_map/ppermute | solution.py:576
  42.7 1.3 %collective-permute-done.3.from_east = f32[152,128]{1,0:T(8,128)S(1)} collective-permute-done((f32[152,128]{1,0:T(8,128)S(1)}, f32[152,128]{1,0:T(8,128)S(1)}, u32[]{:S(2)}, u32[]{:S(2)}) %collective-permute-start.3) | collective-permute-done | bytes 77856 | tf_op jit(solution)/shard_map/ppermute | solution.py:577
  43.9 8.7 %all-to-all-done = f32[64,40,128]{2,1,0:T(8,128)S(1)} async-done(((f32[64,40,128]{2,1,0:T(8,128)}), f32[64,40,128]{2,1,0:T(8,128)S(1)}, u32[]{:S(2)}, u32[]{:S(2)}) %all-to-all-start) | async-done | bytes 1310752 | tf_op jit(solution)/shard_map/all_to_all | solution.py:579
  52.6 20.2 %ocean.1 = f32[6,2,64,256]{3,2,1,0:T(8,128)} custom-call(f32[6]{0:T(128)} %diffusivity_at.1, f32[6]{0:T(128)} %penetration_at.1, f32[4,8]{1,0:T(4,128)} %bitcast.13, bf16[128,2048]{1,0:T(8,128)(2,1)} %constant.4.clone.widen_at, bf16[512,512]{1,0:T(8,128)(2,1)} %constant.5.clone.spread_own_at, s32[64,256]{1,0:T(8,128)} %mask.3, f32[6,2,64,256]{3,2,1,0:T(8,128)} %bitcast.10, ...), custom_call_target="tpu_custom_call" | custom-call | tf_op jit(solution)/shard_map/ocean/pallas_call | solution.py:584
Async XLA Ops:
  2.0 16.0 %collective-permute-start = (f32[19,8,256]{2,1,0:T(8,128)S(1)}, f32[19,8,256]{2,1,0:T(8,128)S(1)}, u32[]{:S(2)}, u32[]{:S(2)}) collective-permute-start(f32[19,8,256]{2,1,0:T(8,128)S(1)} %get-tuple-element.12), channel_id=1, source_target_pairs={{0,16},{16,32},{32,48},{64,80},{80,96},{96,112},{128,144},{144,160... | collective-permute-start | bytes 466952 | tf_op jit(solution)/shard_map/ppermute | solution.py:553
  5.9 12.1 %collective-permute-start.1 = (f32[19,8,256]{2,1,0:T(8,128)S(1)}, f32[19,8,256]{2,1,0:T(8,128)S(1)}, u32[]{:S(2)}, u32[]{:S(2)}) collective-permute-start(f32[19,8,256]{2,1,0:T(8,128)S(1)} %get-tuple-element.13), channel_id=1, source_target_pairs={{16,0},{32,16},{48,32},{80,64},{96,80},{112,96},{144,128},{160,144... | collective-permute-start | bytes 466952 | tf_op jit(solution)/shard_map/ppermute | solution.py:554
  7.2 2.6 %collective-permute-start.4 = (f32[40,128]{1,0:T(8,128)S(1)}, f32[40,128]{1,0:T(8,128)S(1)}, u32[]{:S(2)}, u32[]{:S(2)}) collective-permute-start(f32[40,128]{1,0:T(8,128)S(1)} %get-tuple-element.18.flux), channel_id=1, source_target_pairs={{192,64},{193,65},{194,66},{195,67},{196,68},{197,69},{198,70},{19... | collective-permute-start | bytes 61448 | tf_op jit(solution)/shard_map/ppermute | solution.py:551
  7.9 10.1 %collective-permute-start.5 = (f32[40,128]{1,0:T(8,128)S(1)}, f32[40,128]{1,0:T(8,128)S(1)}, u32[]{:S(2)}, u32[]{:S(2)}) collective-permute-start(f32[40,128]{1,0:T(8,128)S(1)} %get-tuple-element.18.flux), channel_id=1, source_target_pairs={{192,0},{193,1},{194,2},{195,3},{196,4},{197,5},{198,6},{199,7},{2... | collective-permute-start | bytes 61448 | tf_op jit(solution)/shard_map/ppermute | solution.py:551
  9.2 8.8 %collective-permute-start.6 = (f32[40,128]{1,0:T(8,128)S(1)}, f32[40,128]{1,0:T(8,128)S(1)}, u32[]{:S(2)}, u32[]{:S(2)}) collective-permute-start(f32[40,128]{1,0:T(8,128)S(1)} %get-tuple-element.18.flux), channel_id=1, source_target_pairs={{192,128},{193,129},{194,130},{195,131},{196,132},{197,133},{198,1... | collective-permute-start | bytes 61448 | tf_op jit(solution)/shard_map/ppermute | solution.py:551
  19.7 33.0 %all-to-all-start = ((f32[64,40,128]{2,1,0:T(8,128)}), f32[64,40,128]{2,1,0:T(8,128)S(1)}, u32[]{:S(2)}, u32[]{:S(2)}) async-start(f32[64,40,128]{2,1,0:T(8,128)} %payload.1), calls=%async_computation | async-start | bytes 2621440 | tf_op jit(solution)/shard_map/all_to_all | solution.py:579
  31.8 10.8 %collective-permute-start.2 = (f32[152,128]{1,0:T(8,128)S(1)}, f32[152,128]{1,0:T(8,128)S(1)}, u32[]{:S(2)}, u32[]{:S(2)}) collective-permute-start(f32[152,128]{1,0:T(8,128)S(1)} %get-tuple-element.16), channel_id=1, source_target_pairs={{0,1},{1,2},{2,3},{3,4},{4,5},{5,6},{6,7},{7,8},{8,9},{9,10},{10,1... | collective-permute-start | bytes 233480 | tf_op jit(solution)/shard_map/ppermute | solution.py:576
  35.4 8.6 %collective-permute-start.3 = (f32[152,128]{1,0:T(8,128)S(1)}, f32[152,128]{1,0:T(8,128)S(1)}, u32[]{:S(2)}, u32[]{:S(2)}) collective-permute-start(f32[152,128]{1,0:T(8,128)S(1)} %get-tuple-element.17), channel_id=1, source_target_pairs={{1,0},{2,1},{3,2},{4,3},{5,4},{6,5},{7,6},{8,7},{9,8},{10,9},{11,1... | collective-permute-start | bytes 233480 | tf_op jit(solution)/shard_map/ppermute | solution.py:577

commit v5 on v4

--- a/solution.py
+++ b/solution.py
@@ -548,7 +548,7 @@
         mask_at,
         *[hbm(x) for x in (column_weight, routes.reshape(pairs), dest_row.reshape(pairs), weight_id.reshape(pairs))],
     )
-    sent = [lax.ppermute(flux, "comp", [(3, band)]) for band in (1, 0, 2)]
+    sent = [lax.ppermute(flux, "comp", [(3, band)]) for band in range(3)]
     rows_up = [(c * 4 + i, c * 4 + i + 1) for c in range(3) for i in range(3)]
     from_south = lax.ppermute(to_north, ("comp", "lat"), rows_up)
     from_north = lax.ppermute(to_south, ("comp", "lat"), [(b, a) for a, b in rows_up])

time: 73.2 us -> 70.8 us (0.967)
  the two profiles are of different devices: /device:TPU:1 before, /device:TPU:65 now
where the time goes in v5:
time: 70.8 us; the launch traced here: 70.5 us
  starting transfers between devices  24.6 us (35%)
  Pallas kernels  24 us (34%)
  waiting for transfers between devices  21.8 us (31%)
    pallas_call x1, Pallas kernels, shards(): pl.pallas_call(ocean_kernel, out_shape=pltpu.HBM((FLD, LEVB, ROWS, COLS),...  20.2 us
    all_to_all x1, starting transfers between devices, shards(): lax.all_to_all(payload, ('lat', 'lon'), split_axis=0, concat_axis=0, tile...  12.1 us
    all_to_all x1, waiting for transfers between devices, shards(): lax.all_to_all(payload, ('lat', 'lon'), split_axis=0, concat_axis=0, tile...  8.71 us
    ppermute x3, waiting for transfers between devices, shards(): sent = [lax.ppermute(flux, 'comp', [(3, band)]) for band in range(3)]  6.46 us
    ppermute x1, waiting for transfers between devices, shards(): from_west = lax.ppermute(to_east, ('comp', 'lon'), cols_up)  5.37 us
    ppermute x1, starting transfers between devices, shards(): from_west = lax.ppermute(to_east, ('comp', 'lon'), cols_up)  3.54 us
    ppermute x1, starting transfers between devices, shards(): from_south = lax.ppermute(to_north, ('comp', 'lat'), rows_up)  3.12 us
    ppermute x3, starting transfers between devices, shards(): sent = [lax.ppermute(flux, 'comp', [(3, band)]) for band in range(3)]  2.62 us
  transfers between devices with their start and end apart: 8, of which 4 were waited for; matrix products, arithmetic and copies ran while one was open for 0% of the time, Pallas kernels for 0%

profile of v5, /device:TPU:65, one launch (start us, length us, event | category | flops | bytes accessed | tf_op | source)
XLA Modules:
  0.0 70.5 jit_solution(13084278659250663587)
XLA Ops:
  0.0 2.0 %flux.1 = (f32[40,128]{1,0:T(8,128)S(1)}, f32[19,8,256]{2,1,0:T(8,128)S(1)}, f32[19,8,256]{2,1,0:T(8,128)S(1)}, f32[2,64,128]{2,1,0:T(8,128)S(1)}, f32[2,64,128]{2,1,0:T(8,128)S(1)}) custom-call(f32[6,2,64,256]{3,2,1,0:T(8,128)} %bitcast.9, f32[6,2,64,256]{3,2,1,0:T(8,128)} %bitcast.11, s32[64,256]{1,0:T(8,128)} %mask.3, f32[4,192]{1,0:T(4,128)} %weight.1, ...), custom_call_target="tpu_custom_call" | custom-call | tf_op jit(solution)/shard_map/flux/pallas_call | solution.py:530
  2.0 3.1 %collective-permute-start = (f32[19,8,256]{2,1,0:T(8,128)S(1)}, f32[19,8,256]{2,1,0:T(8,128)S(1)}, u32[]{:S(2)}, u32[]{:S(2)}) collective-permute-start(f32[19,8,256]{2,1,0:T(8,128)S(1)} %get-tuple-element.12), channel_id=1, source_target_pairs={{0,16},{16,32},{32,48},{64,80},{80,96},{96,112},{128,144},{144,160... | collective-permute-start | bytes 466952 | tf_op jit(solution)/shard_map/ppermute | solution.py:553
  5.1 1.3 %collective-permute-start.1 = (f32[19,8,256]{2,1,0:T(8,128)S(1)}, f32[19,8,256]{2,1,0:T(8,128)S(1)}, u32[]{:S(2)}, u32[]{:S(2)}) collective-permute-start(f32[19,8,256]{2,1,0:T(8,128)S(1)} %get-tuple-element.13), channel_id=1, source_target_pairs={{16,0},{32,16},{48,32},{80,64},{96,80},{112,96},{144,128},{160,144... | collective-permute-start | bytes 466952 | tf_op jit(solution)/shard_map/ppermute | solution.py:554
  6.4 0.7 collective-permute-start.4
  7.1 1.3 %collective-permute-start.5 = (f32[40,128]{1,0:T(8,128)S(1)}, f32[40,128]{1,0:T(8,128)S(1)}, u32[]{:S(2)}, u32[]{:S(2)}) collective-permute-start(f32[40,128]{1,0:T(8,128)S(1)} %get-tuple-element.18.flux), channel_id=1, source_target_pairs={{192,64},{193,65},{194,66},{195,67},{196,68},{197,69},{198,70},{19... | collective-permute-start | bytes 61448 | tf_op jit(solution)/shard_map/ppermute | solution.py:551
  8.4 0.7 collective-permute-start.6
  9.0 0.0 collective-permute-done.4.first
  9.1 6.5 %collective-permute-done.5.second = f32[40,128]{1,0:T(8,128)S(1)} collective-permute-done((f32[40,128]{1,0:T(8,128)S(1)}, f32[40,128]{1,0:T(8,128)S(1)}, u32[]{:S(2)}, u32[]{:S(2)}) %collective-permute-start.5) | collective-permute-done | bytes 20512 | tf_op jit(solution)/shard_map/ppermute | solution.py:551
  15.5 0.0 collective-permute-done.6.third
  15.5 0.0 collective-permute-done.from_south.south
  15.5 0.0 collective-permute-done.1.from_north.north
  15.5 1.7 %payload.1 = f32[64,40,128]{2,1,0:T(8,128)} custom-call(f32[40,128]{1,0:T(8,128)S(1)} %get-tuple-element.18.flux, f32[40,128]{1,0:T(8,128)S(1)} %collective-permute-done.4.first, f32[40,128]{1,0:T(8,128)S(1)} %collective-permute-done.5.second, f32[40,128]{1,0:T(8,128)S(1)} %collective-permute-done.6.third, ...), custom_call_target="tpu_custom_call" | custom-call | tf_op jit(solution)/shard_map/payload/pallas_call | solution.py:556
  17.2 12.1 %all-to-all-start = ((f32[64,40,128]{2,1,0:T(8,128)}), f32[64,40,128]{2,1,0:T(8,128)S(1)}, u32[]{:S(2)}, u32[]{:S(2)}) async-start(f32[64,40,128]{2,1,0:T(8,128)} %payload.1), calls=%async_computation | async-start | bytes 2621440 | tf_op jit(solution)/shard_map/all_to_all | solution.py:579
  29.3 0.1 strips.1
  29.5 3.5 %collective-permute-start.2 = (f32[152,128]{1,0:T(8,128)S(1)}, f32[152,128]{1,0:T(8,128)S(1)}, u32[]{:S(2)}, u32[]{:S(2)}) collective-permute-start(f32[152,128]{1,0:T(8,128)S(1)} %get-tuple-element.16), channel_id=1, source_target_pairs={{0,1},{1,2},{2,3},{3,4},{4,5},{5,6},{6,7},{7,8},{8,9},{9,10},{10,1... | collective-permute-start | bytes 233480 | tf_op jit(solution)/shard_map/ppermute | solution.py:576
  33.0 1.9 %collective-permute-start.3 = (f32[152,128]{1,0:T(8,128)S(1)}, f32[152,128]{1,0:T(8,128)S(1)}, u32[]{:S(2)}, u32[]{:S(2)}) collective-permute-start(f32[152,128]{1,0:T(8,128)S(1)} %get-tuple-element.17), channel_id=1, source_target_pairs={{1,0},{2,1},{3,2},{4,3},{5,4},{6,5},{7,6},{8,7},{9,8},{10,9},{11,1... | collective-permute-start | bytes 233480 | tf_op jit(solution)/shard_map/ppermute | solution.py:577
  34.9 5.4 %collective-permute-done.2.from_west = f32[152,128]{1,0:T(8,128)S(1)} collective-permute-done((f32[152,128]{1,0:T(8,128)S(1)}, f32[152,128]{1,0:T(8,128)S(1)}, u32[]{:S(2)}, u32[]{:S(2)}) %collective-permute-start.2) | collective-permute-done | bytes 77856 | tf_op jit(solution)/shard_map/ppermute | solution.py:576
  40.3 1.3 %collective-permute-done.3.from_east = f32[152,128]{1,0:T(8,128)S(1)} collective-permute-done((f32[152,128]{1,0:T(8,128)S(1)}, f32[152,128]{1,0:T(8,128)S(1)}, u32[]{:S(2)}, u32[]{:S(2)}) %collective-permute-start.3) | collective-permute-done | bytes 77856 | tf_op jit(solution)/shard_map/ppermute | solution.py:577
  41.6 8.7 %all-to-all-done = f32[64,40,128]{2,1,0:T(8,128)S(1)} async-done(((f32[64,40,128]{2,1,0:T(8,128)}), f32[64,40,128]{2,1,0:T(8,128)S(1)}, u32[]{:S(2)}, u32[]{:S(2)}) %all-to-all-start) | async-done | bytes 1310752 | tf_op jit(solution)/shard_map/all_to_all | solution.py:579
  50.3 20.2 %ocean.1 = f32[6,2,64,256]{3,2,1,0:T(8,128)} custom-call(f32[6]{0:T(128)} %diffusivity_at.1, f32[6]{0:T(128)} %penetration_at.1, f32[4,8]{1,0:T(4,128)} %bitcast.13, bf16[128,2048]{1,0:T(8,128)(2,1)} %constant.4.clone.widen_at, bf16[512,512]{1,0:T(8,128)(2,1)} %constant.5.clone.spread_own_at, s32[64,256]{1,0:T(8,128)} %mask.3, f32[6,2,64,256]{3,2,1,0:T(8,128)} %bitcast.10, ...), custom_call_target="tpu_custom_call" | custom-call | tf_op jit(solution)/shard_map/ocean/pallas_call | solution.py:584
Async XLA Ops:
  2.0 13.5 %collective-permute-start = (f32[19,8,256]{2,1,0:T(8,128)S(1)}, f32[19,8,256]{2,1,0:T(8,128)S(1)}, u32[]{:S(2)}, u32[]{:S(2)}) collective-permute-start(f32[19,8,256]{2,1,0:T(8,128)S(1)} %get-tuple-element.12), channel_id=1, source_target_pairs={{0,16},{16,32},{32,48},{64,80},{80,96},{96,112},{128,144},{144,160... | collective-permute-start | bytes 466952 | tf_op jit(solution)/shard_map/ppermute | solution.py:553
  5.1 10.4 %collective-permute-start.1 = (f32[19,8,256]{2,1,0:T(8,128)S(1)}, f32[19,8,256]{2,1,0:T(8,128)S(1)}, u32[]{:S(2)}, u32[]{:S(2)}) collective-permute-start(f32[19,8,256]{2,1,0:T(8,128)S(1)} %get-tuple-element.13), channel_id=1, source_target_pairs={{16,0},{32,16},{48,32},{80,64},{96,80},{112,96},{144,128},{160,144... | collective-permute-start | bytes 466952 | tf_op jit(solution)/shard_map/ppermute | solution.py:554
  6.4 2.6 %collective-permute-start.4 = (f32[40,128]{1,0:T(8,128)S(1)}, f32[40,128]{1,0:T(8,128)S(1)}, u32[]{:S(2)}, u32[]{:S(2)}) collective-permute-start(f32[40,128]{1,0:T(8,128)S(1)} %get-tuple-element.18.flux), channel_id=1, source_target_pairs={{192,0},{193,1},{194,2},{195,3},{196,4},{197,5},{198,6},{199,7},{2... | collective-permute-start | bytes 61448 | tf_op jit(solution)/shard_map/ppermute | solution.py:551
  7.1 8.4 %collective-permute-start.5 = (f32[40,128]{1,0:T(8,128)S(1)}, f32[40,128]{1,0:T(8,128)S(1)}, u32[]{:S(2)}, u32[]{:S(2)}) collective-permute-start(f32[40,128]{1,0:T(8,128)S(1)} %get-tuple-element.18.flux), channel_id=1, source_target_pairs={{192,64},{193,65},{194,66},{195,67},{196,68},{197,69},{198,70},{19... | collective-permute-start | bytes 61448 | tf_op jit(solution)/shard_map/ppermute | solution.py:551
  8.4 7.1 %collective-permute-start.6 = (f32[40,128]{1,0:T(8,128)S(1)}, f32[40,128]{1,0:T(8,128)S(1)}, u32[]{:S(2)}, u32[]{:S(2)}) collective-permute-start(f32[40,128]{1,0:T(8,128)S(1)} %get-tuple-element.18.flux), channel_id=1, source_target_pairs={{192,128},{193,129},{194,130},{195,131},{196,132},{197,133},{198,1... | collective-permute-start | bytes 61448 | tf_op jit(solution)/shard_map/ppermute | solution.py:551
  17.2 33.1 %all-to-all-start = ((f32[64,40,128]{2,1,0:T(8,128)}), f32[64,40,128]{2,1,0:T(8,128)S(1)}, u32[]{:S(2)}, u32[]{:S(2)}) async-start(f32[64,40,128]{2,1,0:T(8,128)} %payload.1), calls=%async_computation | async-start | bytes 2621440 | tf_op jit(solution)/shard_map/all_to_all | solution.py:579
  29.5 10.8 %collective-permute-start.2 = (f32[152,128]{1,0:T(8,128)S(1)}, f32[152,128]{1,0:T(8,128)S(1)}, u32[]{:S(2)}, u32[]{:S(2)}) collective-permute-start(f32[152,128]{1,0:T(8,128)S(1)} %get-tuple-element.16), channel_id=1, source_target_pairs={{0,1},{1,2},{2,3},{3,4},{4,5},{5,6},{6,7},{7,8},{8,9},{9,10},{10,1... | collective-permute-start | bytes 233480 | tf_op jit(solution)/shard_map/ppermute | solution.py:576
  33.0 8.6 %collective-permute-start.3 = (f32[152,128]{1,0:T(8,128)S(1)}, f32[152,128]{1,0:T(8,128)S(1)}, u32[]{:S(2)}, u32[]{:S(2)}) collective-permute-start(f32[152,128]{1,0:T(8,128)S(1)} %get-tuple-element.17), channel_id=1, source_target_pairs={{1,0},{2,1},{3,2},{4,3},{5,4},{6,5},{7,6},{8,7},{9,8},{10,9},{11,1... | collective-permute-start | bytes 233480 | tf_op jit(solution)/shard_map/ppermute | solution.py:577
